TPU v7x, 512 devices: a whole 4x8x8 slice. The times are simulated.
512 devices in a mesh: cluster: 64 (over z, y), panel: 8 (over x, core).
Axes of the slice: x: 4, y: 8, z: 8, core: 2. Of those that a mesh axis runs over, the one named last changes fastest.
Arguments:
- inputs: bfloat16 [256, 65536], P('panel', 'cluster'), may hold values from -6 to 6
- local_order: int32 [65536], P('cluster'), may hold values from 0 to 1023, as said below
- run_counts: int32 [64], replicated, may hold values from 1 to 32, 1024 in all
- near_cols: int32 [4096], P('cluster'), may hold values from 0 to 1023, as said below
- near_blocks: bfloat16 [64, 262144], P(None, 'cluster'), may hold values from -0.25 to 0.25
- near_scales: float32 [4096], P('cluster'), may hold values from 0.25 to 4
- leaf_bases: bfloat16 [16, 65536], P(None, 'cluster'), may hold values from -0.75 to 0.75
- local_tiles: float32 [1920, 16, 16], P('cluster')
- cross_tiles: float32 [120, 16, 16], replicated
Outputs:
- near_field: bfloat16 [256, 65536], P('panel', 'cluster')
- top_coeffs: float32 [64, 16, 256], P('cluster', None, 'panel')
- top_factor: float32 [64, 16, 16], P('cluster')
- top_gram: float32 [64, 16, 16], P('cluster')
Inputs may be any that keep to these rules, and one draw needn't show every extreme that they name: `local_order`: each device's 1024 entries are a permutation of 0 .. 1023. `run_counts`: they sum to 1024; the largest is exactly 32. `near_cols`: blocks stand 4 to a row leaf in the order of the row leaves; the first block of a row leaf is its diagonal block; every column leaf lies within 2 leaves of its row leaf.
All inputs are finite; a program needn't handle non-finite values.
Results may differ from a plain program's by a relative error of at most 0.0006.
Values may be sent and summed in bfloat16 or wider, within the bound.
A program may use at most 64 MiB of HBM per device.

v0:
```python
import jax
import jax.numpy as jnp
from jax import lax
from jax.sharding import PartitionSpec as P

LEAF = 64
RANK = 16
NEAR = 4
REACH = 2
CROSS = 4


HIGH = lax.Precision.HIGHEST


def extended_2(cells, sides, width):
    for axis, dim in sides:
        count = lax.axis_size(axis)
        ends = count - 1
        head = lax.slice_in_dim(cells, 0, width, axis=dim)
        tail = lax.slice_in_dim(cells, cells.shape[dim] - width, cells.shape[dim], axis=dim)
        cells = jnp.concatenate(
            [
                lax.ppermute(tail, axis, [(i, (i + 1) % count) for i in range(ends)]),
                cells,
                lax.ppermute(head, axis, [((i + 1) % count, i) for i in range(ends)]),
            ],
            axis=dim,
        )
    return cells


def partner(value, axis, bit):
    return lax.ppermute(value, axis, [(i, i ^ 1 << bit) for i in range(lax.axis_size(axis))])


def run_table(run_counts, points):
    ends = jnp.cumsum(run_counts)
    starts = ends - run_counts
    position = jnp.arange(points, dtype=jnp.int32)
    runs = jnp.sum((ends[None, :] <= position[:, None]).astype(jnp.int32), axis=1)
    picks = (runs[:, None] == jnp.arange(run_counts.shape[0], dtype=jnp.int32)[None, :]).astype(
        jnp.int32
    )
    within = position - jnp.sum(picks * starts[None, :], axis=1)
    return (runs, within)


def flip(mats):
    return jnp.swapaxes(mats, -1, -2)


def merge_nodes(left_r, left_c, right_r, right_c, left_e, right_e):
    left_a = jnp.matmul(left_r, left_e, precision=HIGH)
    right_a = jnp.matmul(right_r, right_e, precision=HIGH)
    gram = jnp.matmul(flip(left_a), left_a, precision=HIGH) + jnp.matmul(
        flip(right_a), right_a, precision=HIGH
    )
    moments = jnp.matmul(flip(left_a), left_c, precision=HIGH) + jnp.matmul(
        flip(right_a), right_c, precision=HIGH
    )
    lower = jnp.linalg.cholesky(gram)
    coeffs = jax.scipy.linalg.solve_triangular(lower, moments, lower=True)
    return (flip(lower), coeffs)


def on_device(
    inputs,
    local_order,
    run_counts,
    near_cols,
    near_blocks,
    near_scales,
    leaf_bases,
    local_tiles,
    cross_tiles,
):
    devices = lax.axis_size("cluster")
    me = lax.axis_index("cluster")
    cols_dev, points = inputs.shape
    leaves = points // LEAF
    capacity = 2 * points // devices
    rim = REACH * LEAF
    runs, within = run_table(run_counts, points)
    ends = jnp.cumsum(run_counts)
    starts = ends - run_counts
    slots = jnp.arange(devices * capacity, dtype=jnp.int32)
    target = slots // capacity
    offset = slots % capacity
    distance = (target - me) % devices
    picks = (distance[:, None] == jnp.arange(devices, dtype=jnp.int32)[None, :]).astype(jnp.int32)
    count_of = jnp.sum(picks * run_counts[None, :], axis=1)
    start_of = jnp.sum(picks * starts[None, :], axis=1)
    valid = offset < count_of
    position = jnp.where(valid, start_of + offset, 0)
    source_rows = local_order[position]
    outgoing = jnp.where(valid[None, :], inputs[:, source_rows], jnp.zeros((), jnp.bfloat16))
    sender = (me - runs) % devices
    received = lax.all_to_all(outgoing, "cluster", split_axis=1, concat_axis=1, tiled=True)
    relaid = received[:, sender * capacity + within]
    extended = extended_2(relaid, (("cluster", 1),), rim)
    bases = leaf_bases.reshape(RANK, leaves, LEAF)
    gram = jnp.einsum("knp,jnp->nkj", bases, bases, preferred_element_type=jnp.float32)
    lower = jnp.linalg.cholesky(gram)
    columns = relaid.reshape(cols_dev, leaves, LEAF)
    moments = jnp.einsum("knp,cnp->nkc", bases, columns, preferred_element_type=jnp.float32)
    factor = flip(lower)
    coeffs = jax.scipy.linalg.solve_triangular(lower, moments, lower=True)
    count = leaves
    start = 0
    while count > 1:
        level = local_tiles[start : start + count]
        factor, coeffs = merge_nodes(
            factor[0::2], coeffs[0::2], factor[1::2], coeffs[1::2], level[0::2], level[1::2]
        )
        start += count
        count //= 2
    leaves_ext = extended.reshape(cols_dev, leaves + 2 * REACH, LEAF)
    local_cols = near_cols - (me * leaves - REACH)
    gathered = jnp.take(leaves_ext, local_cols, axis=1)
    blocks_here = near_cols.shape[0]
    mats = near_blocks.reshape(LEAF, blocks_here, LEAF)
    product = jnp.einsum("kbc,cbr->kbr", gathered, mats, preferred_element_type=jnp.float32)
    product = product * near_scales[None, :, None]
    near_field = (
        product.reshape(cols_dev, leaves, NEAR, LEAF)
        .sum(axis=2)
        .reshape(cols_dev, points)
        .astype(jnp.bfloat16)
    )
    for level_index in range(CROSS):
        other_factor, other_coeffs = partner((factor, coeffs), "cluster", level_index)
        node = me // 2**level_index
        parity = node % 2
        sibling = node + 1 - 2 * parity
        first = 2 * devices - 2 * devices // 2**level_index
        own_tile = lax.dynamic_slice_in_dim(cross_tiles, first + node, 1, 0)
        other_tile = lax.dynamic_slice_in_dim(cross_tiles, first + sibling, 1, 0)
        is_odd = parity == 1
        left_r = jnp.where(is_odd, other_factor, factor)
        right_r = jnp.where(is_odd, factor, other_factor)
        left_c = jnp.where(is_odd, other_coeffs, coeffs)
        right_c = jnp.where(is_odd, coeffs, other_coeffs)
        left_e = jnp.where(is_odd, other_tile, own_tile)
        right_e = jnp.where(is_odd, own_tile, other_tile)
        factor, coeffs = merge_nodes(left_r, left_c, right_r, right_c, left_e, right_e)
    partial_gram = jnp.matmul(coeffs, flip(coeffs), precision=HIGH)
    top_gram = lax.psum(partial_gram, "panel")
    return (near_field, coeffs, factor, top_gram)


def solution(mesh):
    placed = (
        P("panel", "cluster"),
        P("cluster"),
        P(),
        P("cluster"),
        P(None, "cluster"),
        P("cluster"),
        P(None, "cluster"),
        P("cluster", None, None),
        P(),
    )
    return jax.shard_map(
        on_device,
        mesh=mesh,
        in_specs=placed,
        out_specs=(
            P("panel", "cluster"),
            P("cluster", None, "panel"),
            P("cluster", None, None),
            P("cluster", None, None),
        ),
        check_vma=False,
    )
```

profile of v0, /device:TPU:1, one launch (start us, length us, event | category | flops | bytes accessed | tf_op | source)
XLA Modules:
  0.0 227.3 jit_solution(16053971614346188337)
XLA Ops:
  2.0 8.6 %gather_fusion = s32[2048]{0:T(1024)S(1)} fusion(s32[1024]{0:T(1024)S(1)} %copy-done, s32[2048]{0:T(1024)S(1)} %broadcast_clamp_fusion), kind=kCustom, calls=%fused_computation | custom fusion | bytes 24576 | tf_op jit(solution)/shard_map/gather | solution.py:96
  10.7 0.8 copy-done.5
  11.6 6.2 %gather_fusion.1 = bf16[2048,32]{1,0:T(8,128)(2,1)S(1)} fusion(bf16[32,1024]{0,1:T(8,128)(2,1)S(1)} %copy.277, s32[2048]{0:T(1024)S(1)} %broadcast_clamp_fusion.1), kind=kCustom, calls=%fused_computation.1 | custom fusion | bytes 270336 | tf_op jit(solution)/shard_map/gather | solution.py:97
  18.1 1.1 reshape.378
  19.2 17.3 %all-to-all-start = ((bf16[64,2,512]{2,1,0:T(2,128)(2,1)}), bf16[64,2,512]{2,1,0:T(2,128)(2,1)S(1)}, u32[]{:S(2)}, u32[]{:S(2)}) async-start(bf16[64,2,512]{2,1,0:T(2,128)(2,1)} %reshape.378), calls=%async_computation | async-start | bytes 262144 | tf_op jit(solution)/shard_map/all_to_all | solution.py:99
  40.7 23.5 %custom-call.38 = f32[16,16,16]{2,1,0:T(8,128)S(1)} custom-call(f32[16,16,16]{2,1,0:T(8,128)S(1)} %fusion.9), custom_call_target="Cholesky" | custom-call | tf_op jit(solution)/shard_map/jit(cholesky)/cholesky | solution.py:104
  65.9 11.7 %custom-call.39 = f32[8,16,16]{2,1,0:T(8,128)S(1)} custom-call(f32[8,16,16]{2,1,0:T(8,128)S(1)} %fusion.13), custom_call_target="Cholesky" | custom-call | tf_op jit(solution)/shard_map/jit(cholesky)/cholesky | solution.py:62
  78.9 5.9 %custom-call.40 = f32[4,16,16]{2,1,0:T(8,128)S(1)} custom-call(f32[4,16,16]{2,1,0:T(8,128)S(1)} %fusion.29), custom_call_target="Cholesky" | custom-call | tf_op jit(solution)/shard_map/jit(cholesky)/cholesky | solution.py:62
  86.0 2.9 %custom-call.41 = f32[2,16,16]{2,1,0:T(8,128)S(1)} custom-call(f32[2,16,16]{2,1,0:T(8,128)S(1)} %fusion.43), custom_call_target="Cholesky" | custom-call | tf_op jit(solution)/shard_map/jit(cholesky)/cholesky | solution.py:62
  90.4 1.5 custom-call.54
  92.5 0.6 fusion.134
  93.1 2.9 %collective-permute-start.2 = (f32[1,16,16]{1,2,0:T(8,128)S(1)}, f32[1,16,16]{1,2,0:T(8,128)S(1)}, u32[]{:S(2)}, u32[]{:S(2)}) collective-permute-start(f32[1,16,16]{1,2,0:T(8,128)S(1)} %get-tuple-element.59), channel_id=1, source_target_pairs={{0,8},{8,0},{16,24},{24,16},{32,40},{40,32},{48,56},{56,48},{64,72... | collective-permute-start | bytes 3080 | tf_op jit(solution)/shard_map/ppermute | solution.py:34
  98.6 1.5 custom-call.55
  100.7 0.6 fusion.135
  101.4 4.0 %collective-permute-start.3 = (f32[1,16,16]{1,2,0:T(8,128)S(1)}, f32[1,16,16]{1,2,0:T(8,128)S(1)}, u32[]{:S(2)}, u32[]{:S(2)}) collective-permute-start(f32[1,16,16]{1,2,0:T(8,128)S(1)} %get-tuple-element.57), channel_id=1, source_target_pairs={{0,16},{8,24},{16,0},{24,8},{32,48},{40,56},{48,32},{56,40},{64,80... | collective-permute-start | bytes 3080 | tf_op jit(solution)/shard_map/ppermute | solution.py:34
  105.8 0.9 collective-permute-done.3
  107.6 1.5 custom-call.56
  109.7 0.6 fusion.136
  110.4 6.7 %collective-permute-start.4 = (f32[1,16,16]{1,2,0:T(8,128)S(1)}, f32[1,16,16]{1,2,0:T(8,128)S(1)}, u32[]{:S(2)}, u32[]{:S(2)}) collective-permute-start(f32[1,16,16]{1,2,0:T(8,128)S(1)} %get-tuple-element.55), channel_id=1, source_target_pairs={{0,32},{8,40},{16,48},{24,56},{32,0},{40,8},{48,16},{56,24},{64,96... | collective-permute-start | bytes 3080 | tf_op jit(solution)/shard_map/ppermute | solution.py:34
  117.1 19.8 %custom-call.45 = f32[16,1,16,16]{2,3,1,0:T(8,128)S(1)} custom-call(f32[16,1,16,16]{3,2,1,0:T(8,128)S(1)} %get-tuple-element.32), custom_call_target="InvertDiagBlocksLowerTriangular" | custom-call | tf_op jit(solution)/shard_map/jit(_solve_triangular)/vmap()/triangular_solve | solution.py:108
  138.2 1.5 custom-call.57
  140.3 0.6 fusion.137
  141.0 3.3 %collective-permute-start.5 = (f32[1,16,16]{1,2,0:T(8,128)S(1)}, f32[1,16,16]{1,2,0:T(8,128)S(1)}, u32[]{:S(2)}, u32[]{:S(2)}) collective-permute-start(f32[1,16,16]{1,2,0:T(8,128)S(1)} %get-tuple-element.53), channel_id=1, source_target_pairs={{0,64},{8,72},{16,80},{24,88},{32,96},{40,104},{48,112},{56,120},{... | collective-permute-start | bytes 3080 | tf_op jit(solution)/shard_map/ppermute | solution.py:34
  144.3 9.8 %custom-call.44 = f32[8,1,16,16]{2,3,1,0:T(8,128)S(1)} custom-call(f32[8,1,16,16]{3,2,1,0:T(8,128)S(1)} %get-tuple-element.44), custom_call_target="InvertDiagBlocksLowerTriangular" | custom-call | tf_op jit(solution)/shard_map/jit(_solve_triangular)/vmap()/triangular_solve | solution.py:63
  154.1 5.0 %custom-call.43 = f32[4,1,16,16]{2,3,1,0:T(8,128)S(1)} custom-call(f32[4,1,16,16]{3,2,1,0:T(8,128)S(1)} %get-tuple-element.46), custom_call_target="InvertDiagBlocksLowerTriangular" | custom-call | tf_op jit(solution)/shard_map/jit(_solve_triangular)/vmap()/triangular_solve | solution.py:63
  159.1 2.5 %custom-call.42 = f32[2,1,16,16]{2,3,1,0:T(8,128)S(1)} custom-call(f32[2,1,16,16]{3,2,1,0:T(8,128)S(1)} %get-tuple-element.48), custom_call_target="InvertDiagBlocksLowerTriangular" | custom-call | tf_op jit(solution)/shard_map/jit(_solve_triangular)/vmap()/triangular_solve | solution.py:63
  161.6 1.2 custom-call.59
  163.3 1.1 reshape.340
  164.4 1.2 custom-call.60
  165.6 1.2 custom-call.61
  166.8 1.2 custom-call.62
  169.0 1.5 custom-call.58
  170.8 3.2 %gather_fusion.2 = bf16[1024,32]{1,0:T(8,128)(2,1)S(1)} fusion(bf16[32,2048]{0,1:T(8,128)(2,1)S(1)} %bitcast.375, s32[1024]{0:T(1024)S(1)} %broadcast_clamp_fusion.2), kind=kCustom, calls=%fused_computation.2 | custom fusion | bytes 135168 | tf_op jit(solution)/shard_map/gather | solution.py:100
  177.5 2.5 %collective-permute-start.6 = (f32[1,16,32]{2,1,0:T(8,128)S(1)}, f32[1,16,32]{2,1,0:T(8,128)S(1)}, u32[]{:S(2)}, u32[]{:S(2)}) collective-permute-start(f32[1,16,32]{2,1,0:T(8,128)S(1)} %convolution_bitcast_fusion.4), channel_id=1, source_target_pairs={{0,8},{8,0},{16,24},{24,16},{32,40},{40,32},{48,56},{56,48},{64,72... | collective-permute-start | bytes 6152 | tf_op jit(solution)/shard_map/ppermute | solution.py:34
  180.6 1.2 collective-permute-done.6
  182.5 2.2 collective-permute-start.7
  184.7 0.7 fusion.177
  185.3 0.7 copy.348
  186.0 1.2 custom-call.63
  188.4 3.8 %collective-permute-start.8 = (f32[1,16,32]{2,1,0:T(8,128)S(1)}, f32[1,16,32]{2,1,0:T(8,128)S(1)}, u32[]{:S(2)}, u32[]{:S(2)}) collective-permute-start(f32[1,16,32]{2,1,0:T(8,128)S(1)} %convolution_bitcast_fusion.2), channel_id=1, source_target_pairs={{0,32},{8,40},{16,48},{24,56},{32,0},{40,8},{48,16},{56,24},{64,96... | collective-permute-start | bytes 6152 | tf_op jit(solution)/shard_map/ppermute | solution.py:34
  192.3 2.8 %collective-permute-start = (bf16[32,128]{0,1:T(8,128)(2,1)S(1)}, bf16[32,128]{0,1:T(8,128)(2,1)S(1)}, u32[]{:S(2)}, u32[]{:S(2)}) collective-permute-start(bf16[32,128]{0,1:T(8,128)(2,1)S(1)} %get-tuple-element.30), channel_id=1, source_target_pairs={{0,8},{8,16},{16,24},{24,32},{32,40},{40,48},{48,56},{56,64},{64,7... | collective-permute-start | bytes 24584 | tf_op jit(solution)/shard_map/ppermute | solution.py:24
  195.1 1.3 collective-permute-start.1
  197.3 5.2 %collective-permute-start.9 = (f32[1,16,32]{2,1,0:T(8,128)S(1)}, f32[1,16,32]{2,1,0:T(8,128)S(1)}, u32[]{:S(2)}, u32[]{:S(2)}) collective-permute-start(f32[1,16,32]{2,1,0:T(8,128)S(1)} %convolution_bitcast_fusion.1), channel_id=1, source_target_pairs={{0,64},{8,72},{16,80},{24,88},{32,96},{40,104},{48,112},{56,120},{... | collective-permute-start | bytes 6152 | tf_op jit(solution)/shard_map/ppermute | solution.py:34
  202.9 0.9 collective-permute-done.9
  205.1 19.1 %psum.7 = f32[1,16,16]{2,1,0:T(8,128)} all-reduce(f32[1,16,16]{2,1,0:T(8,128)S(1)} %convolution_bitcast_fusion), channel_id=1, replica_groups=mesh['cluster'=64,'panel'=8] {'panel'}, use_global_device_ids=true, to_apply=%region_16.19 | all-reduce | flops 256 | bytes 2048 | tf_op jit(solution)/shard_map/psum | solution.py:148
  224.2 0.7 gather_fusion.3
  225.5 0.9 bitcast_reduce_fusion
  226.5 0.8 convert_element_type.13
  (185 shorter events, 29.8 us)
Async XLA Ops:
  0.6 1.4 copy-start
  0.7 0.7 copy-start.7
  10.6 0.8 copy-start.5
  19.2 17.3 %copy-start.2 = (f32[30,16,16]{0,2,1:T(8,128)S(1)}, f32[30,16,16]{0,2,1:T(8,128)}, u32[]{:S(2)}) copy-start(f32[30,16,16]{0,2,1:T(8,128)} %param.19) | copy-start | bytes 92164
  19.2 151.3 %all-to-all-start = ((bf16[64,2,512]{2,1,0:T(2,128)(2,1)}), bf16[64,2,512]{2,1,0:T(2,128)(2,1)S(1)}, u32[]{:S(2)}, u32[]{:S(2)}) async-start(bf16[64,2,512]{2,1,0:T(2,128)(2,1)} %reshape.378), calls=%async_computation | async-start | bytes 262144 | tf_op jit(solution)/shard_map/all_to_all | solution.py:99
  38.8 0.8 copy-start.6
  93.1 4.6 %collective-permute-start.2 = (f32[1,16,16]{1,2,0:T(8,128)S(1)}, f32[1,16,16]{1,2,0:T(8,128)S(1)}, u32[]{:S(2)}, u32[]{:S(2)}) collective-permute-start(f32[1,16,16]{1,2,0:T(8,128)S(1)} %get-tuple-element.59), channel_id=1, source_target_pairs={{0,8},{8,0},{16,24},{24,16},{32,40},{40,32},{48,56},{56,48},{64,72... | collective-permute-start | bytes 3080 | tf_op jit(solution)/shard_map/ppermute | solution.py:34
  96.1 0.9 copy-start.1
  101.4 4.0 %copy-start.8 = (s32[64]{0:T(128)S(1)}, s32[64]{0:T(128)}, u32[]{:S(2)}) copy-start(s32[64]{0:T(128)} %param.15) | copy-start | bytes 772
  101.4 5.3 %collective-permute-start.3 = (f32[1,16,16]{1,2,0:T(8,128)S(1)}, f32[1,16,16]{1,2,0:T(8,128)S(1)}, u32[]{:S(2)}, u32[]{:S(2)}) collective-permute-start(f32[1,16,16]{1,2,0:T(8,128)S(1)} %get-tuple-element.57), channel_id=1, source_target_pairs={{0,16},{8,24},{16,0},{24,8},{32,48},{40,56},{48,32},{56,40},{64,80... | collective-permute-start | bytes 3080 | tf_op jit(solution)/shard_map/ppermute | solution.py:34
  107.3 56.0 %copy-start.3 = (bf16[64,4096]{1,0:T(8,128)(2,1)S(1)}, bf16[64,4096]{1,0:T(8,128)(2,1)}, u32[]{:S(2)}) copy-start(bf16[64,4096]{1,0:T(8,128)(2,1)} %param.16) | copy-start | bytes 1572868
  110.4 26.9 %collective-permute-start.4 = (f32[1,16,16]{1,2,0:T(8,128)S(1)}, f32[1,16,16]{1,2,0:T(8,128)S(1)}, u32[]{:S(2)}, u32[]{:S(2)}) collective-permute-start(f32[1,16,16]{1,2,0:T(8,128)S(1)} %get-tuple-element.55), channel_id=1, source_target_pairs={{0,32},{8,40},{16,48},{24,56},{32,0},{40,8},{48,16},{56,24},{64,96... | collective-permute-start | bytes 3080 | tf_op jit(solution)/shard_map/ppermute | solution.py:34
  141.0 27.1 %collective-permute-start.5 = (f32[1,16,16]{1,2,0:T(8,128)S(1)}, f32[1,16,16]{1,2,0:T(8,128)S(1)}, u32[]{:S(2)}, u32[]{:S(2)}) collective-permute-start(f32[1,16,16]{1,2,0:T(8,128)S(1)} %get-tuple-element.53), channel_id=1, source_target_pairs={{0,64},{8,72},{16,80},{24,88},{32,96},{40,104},{48,112},{56,120},{... | collective-permute-start | bytes 3080 | tf_op jit(solution)/shard_map/ppermute | solution.py:34
  177.5 4.4 %collective-permute-start.6 = (f32[1,16,32]{2,1,0:T(8,128)S(1)}, f32[1,16,32]{2,1,0:T(8,128)S(1)}, u32[]{:S(2)}, u32[]{:S(2)}) collective-permute-start(f32[1,16,32]{2,1,0:T(8,128)S(1)} %convolution_bitcast_fusion.4), channel_id=1, source_target_pairs={{0,8},{8,0},{16,24},{24,16},{32,40},{40,32},{48,56},{56,48},{64,72... | collective-permute-start | bytes 6152 | tf_op jit(solution)/shard_map/ppermute | solution.py:34
  182.5 5.3 %collective-permute-start.7 = (f32[1,16,32]{2,1,0:T(8,128)S(1)}, f32[1,16,32]{2,1,0:T(8,128)S(1)}, u32[]{:S(2)}, u32[]{:S(2)}) collective-permute-start(f32[1,16,32]{2,1,0:T(8,128)S(1)} %convolution_bitcast_fusion.3), channel_id=1, source_target_pairs={{0,16},{8,24},{16,0},{24,8},{32,48},{40,56},{48,32},{56,40},{64,80... | collective-permute-start | bytes 6152 | tf_op jit(solution)/shard_map/ppermute | solution.py:34
  188.4 8.3 %collective-permute-start.8 = (f32[1,16,32]{2,1,0:T(8,128)S(1)}, f32[1,16,32]{2,1,0:T(8,128)S(1)}, u32[]{:S(2)}, u32[]{:S(2)}) collective-permute-start(f32[1,16,32]{2,1,0:T(8,128)S(1)} %convolution_bitcast_fusion.2), channel_id=1, source_target_pairs={{0,32},{8,40},{16,48},{24,56},{32,0},{40,8},{48,16},{56,24},{64,96... | collective-permute-start | bytes 6152 | tf_op jit(solution)/shard_map/ppermute | solution.py:34
  192.3 10.2 %collective-permute-start = (bf16[32,128]{0,1:T(8,128)(2,1)S(1)}, bf16[32,128]{0,1:T(8,128)(2,1)S(1)}, u32[]{:S(2)}, u32[]{:S(2)}) collective-permute-start(bf16[32,128]{0,1:T(8,128)(2,1)S(1)} %get-tuple-element.30), channel_id=1, source_target_pairs={{0,8},{8,16},{16,24},{24,32},{32,40},{40,48},{48,56},{56,64},{64,7... | collective-permute-start | bytes 24584 | tf_op jit(solution)/shard_map/ppermute | solution.py:24
  195.1 7.5 %collective-permute-start.1 = (bf16[32,128]{0,1:T(8,128)(2,1)S(1)}, bf16[32,128]{0,1:T(8,128)(2,1)S(1)}, u32[]{:S(2)}, u32[]{:S(2)}) collective-permute-start(bf16[32,128]{0,1:T(8,128)(2,1)S(1)} %get-tuple-element.31), channel_id=1, source_target_pairs={{8,0},{16,8},{24,16},{32,24},{40,32},{48,40},{56,48},{64,56},{72,6... | collective-permute-start | bytes 24584 | tf_op jit(solution)/shard_map/ppermute | solution.py:26
  197.3 6.6 %collective-permute-start.9 = (f32[1,16,32]{2,1,0:T(8,128)S(1)}, f32[1,16,32]{2,1,0:T(8,128)S(1)}, u32[]{:S(2)}, u32[]{:S(2)}) collective-permute-start(f32[1,16,32]{2,1,0:T(8,128)S(1)} %convolution_bitcast_fusion.1), channel_id=1, source_target_pairs={{0,64},{8,72},{16,80},{24,88},{32,96},{40,104},{48,112},{56,120},{... | collective-permute-start | bytes 6152 | tf_op jit(solution)/shard_map/ppermute | solution.py:34
  204.5 0.6 copy-start.4
  224.9 0.7 copy-start.9
where the time goes:
time: 228 us; the launch traced here: 227 us
  other arithmetic  103 us (45%)
  starting transfers between devices  52 us (23%)
  local copies, waits for them, and re-layouts  33.3 us (15%)
  blocking collectives  19.1 us (8%)
  matrix products  14.1 us (6%)
  waiting for transfers between devices  3.9 us (2%)
    another operation x25, other arithmetic, merge_nodes(): lower = jnp.linalg.cholesky(gram)  31.7 us
    ppermute x8, starting transfers between devices, partner(): lax.ppermute(value, axis, [(i, i ^ 1 << bit) for i in range(lax.axis_size...  30.6 us
    another operation x15, other arithmetic, merge_nodes(): coeffs = jax.scipy.linalg.solve_triangular(lower, moments, lower=True)  26.3 us
    another operation x2, other arithmetic, on_device(): lower = jnp.linalg.cholesky(gram)  23.5 us
    another operation x2, other arithmetic, on_device(): coeffs = jax.scipy.linalg.solve_triangular(lower, moments, lower=True)  19.9 us
    psum x1, blocking collectives, on_device(): top_gram = lax.psum(partial_gram, 'panel')  19.1 us
    all_to_all x1, starting transfers between devices, on_device(): lax.all_to_all(outgoing, 'cluster', split_axis=1, concat_axis=1, tiled=True)  17.3 us
    unnamed x40, local copies, waits for them, and re-layouts  8.6 us
  transfers between devices with their start and end apart: 11, of which 5 were waited for; matrix products, arithmetic and copies ran while one was open for 52% of the time, Pallas kernels for 0%

commit v1 on v0

v1 whole, which is shorter than its diff:
```python
import functools

import jax
import jax.numpy as jnp
from jax import lax
from jax.experimental import pallas as pl
from jax.experimental.pallas import tpu as pltpu
from jax.sharding import PartitionSpec as P

LEAF = 64
RANK = 16
NEAR = 4
REACH = 2
CROSS = 4
CAP = 32
LANES = 128
MESH = pl.DeviceIdType.MESH
HIGH = lax.Precision.HIGHEST
F32 = jnp.float32
BF16 = jnp.bfloat16


def iota(shape, dim):
    return lax.broadcasted_iota(jnp.int32, shape, dim)


def dot(a, b, precision=None):
    return lax.dot_general(
        a, b, (((1,), (0,)), ((), ())), precision=precision, preferred_element_type=F32
    )


def dot_t(a, b, precision=None):
    return lax.dot_general(
        a, b, (((1,), (1,)), ((), ())), precision=precision, preferred_element_type=F32
    )


def split3(x):
    hi = x.astype(BF16)
    rest = x - hi.astype(F32)
    mid = rest.astype(BF16)
    low = (rest - mid.astype(F32)).astype(BF16)
    return hi, mid, low


def group_sum(x, width):
    shift = LANES // 2
    while shift >= width:
        x = x + pltpu.roll(x, shift, 1)
        shift //= 2
    return x


def pack2(x):
    keep = iota((RANK, LANES), 0) % 8 == iota((RANK, LANES), 1) // RANK
    return jnp.where(keep, x, 0.0).reshape(2, 8, LANES).sum(axis=1)


def unpack2(x):
    rows = jnp.concatenate(
        [jnp.broadcast_to(x[0:1], (8, LANES)), jnp.broadcast_to(x[1:2], (8, LANES))], axis=0
    )
    keep = iota((RANK, LANES), 0) % 8 == iota((RANK, LANES), 1) // RANK
    return group_sum(jnp.where(keep, rows, 0.0), RANK)


def body(
    devices, panels, x_ref, order_ref, counts_ref, countv_ref, cols_ref, scales_ref, mats_hbm,
    bases_ref, local_hbm, cross_hbm, near_ref, coeffs_ref, factor_ref, topgram_ref,
    mats, local_v, cross_v, sorted_ref, out, recv, own, ext, moment_out, moment_in, gram_out, gram_in,
    top_out, top_in, hot_ref, quarter_ref,
    mats_sem, local_sem, cross_sem, a2a_send, a2a_recv, gram_send, gram_recv, moment_send, moment_recv,
    top_send, top_recv, left_send, left_recv, right_send, right_recv,
):
    me = lax.axis_index("cluster")
    panel = lax.axis_index("panel")
    group = 2**CROSS
    rank_in = lax.rem(me, group)
    base = me - rank_in
    channels, points = x_ref.shape
    leaves = points // LEAF

    load_mats = pltpu.make_async_copy(mats_hbm, mats, mats_sem)
    load_local = pltpu.make_async_copy(local_hbm, local_v, local_sem)
    load_cross = pltpu.make_async_copy(cross_hbm, cross_v, cross_sem)
    load_local.start()
    load_cross.start()
    load_mats.start()

    barrier = pltpu.get_barrier_semaphore()

    def greet(m, carry):
        pl.semaphore_signal(
            barrier, 1, device_id=(lax.rem(me + m, devices), panel), device_id_type=MESH
        )
        return carry

    lax.fori_loop(1, devices, greet, 0, unroll=9)

    def greet_panel(m, carry):
        pl.semaphore_signal(
            barrier, 1, device_id=(me, lax.rem(panel + m, panels)), device_id_type=MESH
        )
        return carry

    lax.fori_loop(1, panels, greet_panel, 0, unroll=7)

    x4 = jnp.concatenate([x_ref[...]] * 4, axis=0)
    point = iota((LANES, points), 1)
    hots = []
    for b in range(points // LANES):
        row = jnp.broadcast_to(order_ref[b : b + 1, :], (LANES, LANES))
        col = jnp.concatenate([row.T] * (points // LANES), axis=1)
        hots.append((col == point).astype(F32).astype(BF16))
    sorted_ref[pl.ds(0, points), :] = dot_t(jnp.concatenate(hots, axis=0), x4)
    sorted_ref[pl.ds(points, CAP), :] = jnp.zeros((CAP, LANES), F32)

    part = iota((8, LANES), 1) // channels

    def fill(m, start):
        rows = [sorted_ref[pl.ds(start + 8 * q, 8), :] for q in range(4)]
        low = jnp.where(part == 0, rows[0], rows[1])
        high = jnp.where(part == 2, rows[2], rows[3])
        out[m] = jnp.where(part < 2, low, high).astype(BF16)
        return start + counts_ref[m]

    lax.fori_loop(0, devices, fill, 0, unroll=8)

    pl.semaphore_wait(barrier, devices - 1 + panels - 1)

    def send(m, carry):
        pltpu.make_async_remote_copy(
            out.at[m], recv.at[m], a2a_send, a2a_recv,
            device_id=(lax.rem(me + m, devices), panel), device_id_type=MESH,
        ).start()
        return carry

    lax.fori_loop(1, devices, send, 0, unroll=9)
    recv[0] = out[0]

    load_local.wait()
    load_cross.wait()
    tiles = local_v.shape[2]
    lane = iota((tiles, LANES), 1)
    leaf = lane % leaves
    want = jnp.where(
        lane < leaves, leaf,
        jnp.where(
            lane < 2 * leaves, 16 + leaf // 2,
            jnp.where(lane < 3 * leaves, 24 + leaf // 4, 28 + leaf // 8),
        ),
    )
    pick_local = ((iota((tiles, LANES), 0) == want) & (lane < 4 * leaves)).astype(F32).astype(BF16)
    tiles_x = cross_v.shape[2]
    lane = iota((tiles_x, LANES), 1)
    level = lane // leaves - 4
    firsts = [2 * devices - 2 * devices // 2**t + me // 2**t for t in range(CROSS)]
    want = jnp.where(
        level == 0, firsts[0],
        jnp.where(level == 1, firsts[1], jnp.where(level == 2, firsts[2], firsts[3])),
    )
    pick_cross = ((iota((tiles_x, LANES), 0) == want) & (level >= 0)).astype(F32).astype(BF16)
    chain = jnp.zeros((RANK * RANK, LANES), F32)
    for source, pick in ((local_v, pick_local), (cross_v, pick_cross)):
        flat = source[...].reshape(RANK * RANK, source.shape[2])
        for term in split3(flat):
            chain = chain + dot(term, pick)
    for step in (leaves, 2 * leaves, 4 * leaves):
        left = chain.reshape(RANK, RANK, LANES)
        right = pltpu.roll(chain, LANES - step, 1).reshape(RANK, RANK, LANES)
        total = left[:, 0:1, :] * right[0:1]
        for k in range(1, RANK):
            total = total + left[:, k : k + 1, :] * right[k : k + 1]
        chain = total.reshape(RANK * RANK, LANES)
    hi, mid, low = split3(chain)
    lane = iota((RANK * RANK, LANES), 1)
    terms = jnp.where(
        lane < leaves, hi.astype(F32),
        jnp.where(
            lane < 2 * leaves, pltpu.roll(mid.astype(F32), leaves, 1),
            jnp.where(lane < 3 * leaves, pltpu.roll(low.astype(F32), 2 * leaves, 1), 0.0),
        ),
    ).astype(BF16)
    spread = iota((LANES, points), 0)
    spread = ((spread % leaves == iota((LANES, points), 1) // LEAF) & (spread < 3 * leaves))
    path = dot(terms, spread.astype(F32).astype(BF16)).reshape(RANK, RANK, points)
    bases = bases_ref[...].astype(F32)
    weights = path[0] * bases[0:1]
    for k in range(1, RANK):
        weights = weights + path[k] * bases[k : k + 1]
    parts = split3(weights)
    weights3 = jnp.concatenate(parts, axis=0)

    wide = jnp.concatenate([p for p in parts for _ in range(8)], axis=0)
    gram = dot_t(weights3, wide)
    gram = gram[0:RANK] + gram[RANK : 2 * RANK] + gram[2 * RANK :]
    gram = gram[:, 0:LANES] + gram[:, LANES : 2 * LANES] + gram[:, 2 * LANES :]
    packed = pack2(gram)
    gram_out[...] = packed
    gram_in[rank_in] = packed

    def send_gram(m, carry):
        pltpu.make_async_remote_copy(
            gram_out, gram_in.at[rank_in], gram_send, gram_recv,
            device_id=(base + lax.rem(rank_in + m, group), panel), device_id_type=MESH,
        ).start()
        return carry

    lax.fori_loop(1, group, send_gram, 0, unroll=15)

    counts = countv_ref[...].astype(F32)
    square = (devices, devices)
    upto = (iota(square, 0) <= iota(square, 1)).astype(F32).astype(BF16)
    ends = dot(jnp.broadcast_to(counts, (8, devices)).astype(BF16), upto)[0:1]
    diagonal = jnp.where(iota(square, 0) == iota(square, 1), jnp.broadcast_to(counts, square), 0.0)
    counts_col = dot(diagonal.astype(BF16), jnp.ones((devices, LANES), BF16))
    both = jnp.concatenate([counts_col, jnp.ones((devices, LANES), F32)], axis=1).astype(BF16)
    position = iota((points, devices), 0).astype(F32)
    passed = dot((ends <= position).astype(F32).astype(BF16), both)
    within = (iota((points, LANES), 0).astype(F32) - passed[:, :LANES]).astype(jnp.int32)
    run = passed[:, LANES:].astype(jnp.int32)
    quarter_ref[...] = (within // 8 == iota((points, LANES), 1) // channels).astype(F32)
    slot = run * 8 + within % 8
    slots = devices * 8
    hot_ref[...] = (
        (jnp.concatenate([slot] * (slots // LANES), axis=1) == iota((points, slots), 1))
        .astype(F32)
        .astype(BF16)
    )

    others = pl.ds(1, devices - 1)
    pltpu.make_async_copy(recv.at[others], recv.at[others], a2a_recv).wait()

    received = recv[...].astype(F32).reshape(slots, LANES).astype(BF16)
    relaid = dot(hot_ref[...], received)
    relaid = jnp.where(quarter_ref[...] > 0.5, relaid, 0.0).astype(BF16)

    moment = dot(weights3, relaid)
    moment = moment[0:RANK] + moment[RANK : 2 * RANK] + moment[2 * RANK :]
    moment = group_sum(moment, channels)
    part = iota((4, LANES), 1) // channels
    low = jnp.where(part == 0, moment[0:4], moment[4:8])
    high = jnp.where(part == 2, moment[8:12], moment[12:16])
    packed = jnp.where(part < 2, low, high)
    moment_out[...] = packed
    moment_in[rank_in] = packed

    def send_moment(m, carry):
        pltpu.make_async_remote_copy(
            moment_out, moment_in.at[rank_in], moment_send, moment_recv,
            device_id=(base + lax.rem(rank_in + m, group), panel), device_id_type=MESH,
        ).start()
        return carry

    lax.fori_loop(1, group, send_moment, 0, unroll=15)

    fold = (iota((channels, LANES), 1) % channels == iota((channels, LANES), 0)).astype(F32).astype(BF16)
    for n in range(leaves):
        columns = dot_t(fold, relaid[n * LEAF : (n + 1) * LEAF]).astype(BF16)
        own[n] = columns
        ext[n + REACH] = columns
    right = lax.rem(me + 1, devices)
    left = lax.rem(me + devices - 1, devices)
    to_left = pltpu.make_async_remote_copy(
        own.at[pl.ds(0, REACH)], ext.at[pl.ds(leaves + REACH, REACH)], left_send, left_recv,
        device_id=(left, panel), device_id_type=MESH,
    )
    to_right = pltpu.make_async_remote_copy(
        own.at[pl.ds(leaves - REACH, REACH)], ext.at[pl.ds(0, REACH)], right_send, right_recv,
        device_id=(right, panel), device_id_type=MESH,
    )
    to_left.start()
    to_right.start()

    peers = pl.ds(0, group - 1)
    pltpu.make_async_copy(gram_in.at[peers], gram_in.at[peers], gram_recv).wait()
    sub = iota((RANK, LANES), 0)
    lane = iota((RANK, LANES), 1)
    tableau = jnp.where(
        lane < RANK, unpack2(jnp.sum(gram_in[...], axis=0)), (lane - RANK == sub).astype(F32)
    )
    for k in range(RANK - 1):
        ratio = tableau[:, k : k + 1] / tableau[k : k + 1, k : k + 1]
        tableau = tableau - jnp.where(sub > k, ratio * tableau[k : k + 1, :], 0.0)
    pivots = jnp.sum(jnp.where(lane == sub, tableau, 0.0), axis=1, keepdims=True)
    tableau = tableau * (1.0 / jnp.sqrt(pivots))
    factor_ref[0] = jnp.where(lane >= sub, tableau, 0.0)[:, :RANK]
    inverse = tableau[:, RANK : 2 * RANK]

    load_mats.wait()

    def near_leaf(i, source, first):
        rows = jnp.concatenate(
            [source[jnp.clip(cols_ref[NEAR * i + t] - first, 0, source.shape[0] - 1)] for t in range(NEAR)],
            axis=0,
        )
        width = NEAR * LEAF
        prod = dot(rows, mats[:, i * width : (i + 1) * width])
        lower = iota((channels, LANES), 1) < LEAF
        halves = []
        for h in range(2):
            cut = prod[:, h * LANES : (h + 1) * LANES]
            halves.append(
                jnp.where(
                    lower,
                    cut[2 * h * channels : (2 * h + 1) * channels] * scales_ref[NEAR * i + 2 * h],
                    cut[(2 * h + 1) * channels : (2 * h + 2) * channels] * scales_ref[NEAR * i + 2 * h + 1],
                )
            )
        both = halves[0] + halves[1]
        return both + pltpu.roll(both, LEAF, 1)

    def near_pair(i, source, first):
        a = near_leaf(i, source, first)
        b = near_leaf(i + 1, source, first)
        lower = iota((channels, LANES), 1) < LEAF
        near_ref[:, i * LEAF : (i + 2) * LEAF] = jnp.where(lower, a, b).astype(BF16)

    for i in range(REACH, leaves - REACH, 2):
        near_pair(i, own, me * leaves)

    pltpu.make_async_copy(moment_in.at[peers], moment_in.at[peers], moment_recv).wait()
    packed = jnp.sum(moment_in[...], axis=0)
    moment = jnp.concatenate(
        [packed[:, q * channels : (q + 1) * channels] for q in range(4)], axis=0
    )
    coeffs = dot(inverse, moment, HIGH)
    coeffs_ref[0] = coeffs
    packed = pack2(dot_t(coeffs, jnp.concatenate([coeffs] * 8, axis=0), HIGH))
    top_out[...] = packed
    top_in[panel] = packed

    def send_top(m, carry):
        pltpu.make_async_remote_copy(
            top_out, top_in.at[panel], top_send, top_recv,
            device_id=(me, lax.rem(panel + m, panels)), device_id_type=MESH,
        ).start()
        return carry

    lax.fori_loop(1, panels, send_top, 0, unroll=7)

    to_left.wait_recv()
    to_right.wait_recv()
    first = me * leaves - REACH
    near_pair(0, ext, first)
    near_pair(leaves - 2, ext, first)

    peers = pl.ds(0, panels - 1)
    pltpu.make_async_copy(top_in.at[peers], top_in.at[peers], top_recv).wait()
    topgram_ref[0] = unpack2(jnp.sum(top_in[...], axis=0))[:, :RANK]

    pltpu.make_async_copy(out.at[others], out.at[others], a2a_send).wait()
    peers = pl.ds(0, group - 1)
    pltpu.make_async_copy(gram_in.at[peers], gram_in.at[peers], gram_send).wait()
    pltpu.make_async_copy(moment_in.at[peers], moment_in.at[peers], moment_send).wait()
    peers = pl.ds(0, panels - 1)
    pltpu.make_async_copy(top_in.at[peers], top_in.at[peers], top_send).wait()
    to_left.wait_send()
    to_right.wait_send()


def on_device(
    inputs, local_order, run_counts, near_cols, near_blocks, near_scales, leaf_bases, local_tiles,
    cross_tiles,
):
    devices = lax.axis_size("cluster")
    panels = lax.axis_size("panel")
    channels, points = inputs.shape
    leaves = points // LEAF
    group = 2**CROSS
    vmem = pl.BlockSpec(memory_space=pltpu.VMEM)
    smem = pl.BlockSpec(memory_space=pltpu.SMEM)
    hbm = pl.BlockSpec(memory_space=pl.ANY)
    local_t = jnp.transpose(local_tiles, (1, 2, 0))
    cross_t = jnp.transpose(cross_tiles, (1, 2, 0))
    dma = pltpu.SemaphoreType.DMA
    return pl.pallas_call(
        functools.partial(body, devices, panels),
        out_shape=(
            jax.ShapeDtypeStruct((channels, points), BF16),
            jax.ShapeDtypeStruct((1, RANK, channels), F32),
            jax.ShapeDtypeStruct((1, RANK, RANK), F32),
            jax.ShapeDtypeStruct((1, RANK, RANK), F32),
        ),
        in_specs=[vmem, vmem, smem, vmem, smem, smem, hbm, vmem, hbm, hbm],
        out_specs=(vmem, vmem, vmem, vmem),
        scratch_shapes=[
            pltpu.VMEM(near_blocks.shape, BF16),
            pltpu.VMEM(local_t.shape, F32),
            pltpu.VMEM(cross_t.shape, F32),
            pltpu.VMEM((points + CAP, LANES), F32),
            pltpu.VMEM((devices, 8, LANES), BF16),
            pltpu.VMEM((devices, 8, LANES), BF16),
            pltpu.VMEM((leaves, channels, LEAF), BF16),
            pltpu.VMEM((leaves + 2 * REACH, channels, LEAF), BF16),
            pltpu.VMEM((4, LANES), F32),
            pltpu.VMEM((group, 4, LANES), F32),
            pltpu.VMEM((2, LANES), F32),
            pltpu.VMEM((group, 2, LANES), F32),
            pltpu.VMEM((2, LANES), F32),
            pltpu.VMEM((panels, 2, LANES), F32),
            pltpu.VMEM((points, devices * 8), BF16),
            pltpu.VMEM((points, LANES), F32),
        ]
        + [dma] * 15,
        compiler_params=pltpu.CompilerParams(
            collective_id=0, has_side_effects=True, vmem_limit_bytes=48 * 2**20
        ),
    )(
        inputs,
        local_order.reshape(points // LANES, LANES),
        run_counts,
        run_counts.reshape(1, devices),
        near_cols,
        near_scales,
        near_blocks,
        leaf_bases,
        local_t,
        cross_t,
    )


def solution(mesh):
    placed = (
        P("panel", "cluster"),
        P("cluster"),
        P(),
        P("cluster"),
        P(None, "cluster"),
        P("cluster"),
        P(None, "cluster"),
        P("cluster", None, None),
        P(),
    )
    return jax.shard_map(
        on_device,
        mesh=mesh,
        in_specs=placed,
        out_specs=(
            P("panel", "cluster"),
            P("cluster", None, "panel"),
            P("cluster", None, None),
            P("cluster", None, None),
        ),
        check_vma=False,
    )
```

time: 228 us -> 45.6 us (0.20)
  other arithmetic: 103 us -> 0 us
  starting transfers between devices: 52 us -> 0 us
  Pallas kernels: 0 us -> 37 us
  local copies, waits for them, and re-layouts: 33.3 us -> 7.54 us
  blocking collectives: 19.1 us -> 0 us
  matrix products: 14.1 us -> 0 us
  waiting for transfers between devices: 3.9 us -> 0 us
    another operation x46 -> x0, other arithmetic: 102 us -> none  [the longest x25 31.7 us: merge_nodes(): lower = jnp.linalg.cholesky(gram)]
    pallas_call x0 -> x1, Pallas kernels: none -> 37 us  [on_device(): pl.pallas_call(functools.partial(body, devices, panels), out_shape=(jax.S...]
    ppermute x10 -> x0, starting transfers between devices: 34.7 us -> none  [the longest x8 30.6 us: partner(): lax.ppermute(value, axis, [(i, i ^ 1 << bit) for i in range(lax.axis_size...]
    psum x1 -> x0, blocking collectives: 19.1 us -> none  [on_device(): top_gram = lax.psum(partial_gram, 'panel')]
    gather x5 -> x0, local copies, waits for them, and re-layouts: 18.8 us -> none  [the longest x1 8.58 us: on_device(): source_rows = local_order[position]]
    all_to_all x1 -> x0, starting transfers between devices: 17.3 us -> none  [on_device(): lax.all_to_all(outgoing, 'cluster', split_axis=1, concat_axis=1, tiled=True)]
    dot_general x52 -> x0, matrix products: 11.9 us -> none  [the longest x8 1.77 us: merge_nodes(): jnp.matmul(flip(left_a), left_a, precision=HIGH)]
    ppermute x10 -> x0, waiting for transfers between devices: 3.9 us -> none  [the longest x8 3.89 us: partner(): lax.ppermute(value, axis, [(i, i ^ 1 << bit) for i in range(lax.axis_size...]
  transfers between devices with their start and end apart: 11 -> 0, of which waited for: 5 -> 0; matrix products, arithmetic and copies ran while one was open for 52% -> 0% of each run, Pallas kernels for 0% -> 0%
where the time goes in v1:
time: 45.6 us; the launch traced here: 45.2 us
  Pallas kernels  37 us (81%)
  local copies, waits for them, and re-layouts  7.54 us (17%)
  between operations  0.68 us (1%)
    pallas_call x1, Pallas kernels, on_device(): pl.pallas_call(functools.partial(body, devices, panels), out_shape=(jax.S...  37 us
    unnamed x22, local copies, waits for them, and re-layouts  7.54 us

profile of v1, /device:TPU:1, one launch (start us, length us, event | category | flops | bytes accessed | tf_op | source)
XLA Modules:
  0.0 45.2 jit_solution(17710634351792616888)
XLA Ops:
  0.6 0.0 copy-start.5
  0.6 0.0 copy-start.6
  0.7 0.0 copy-start.7
  0.7 0.0 copy-start.8
  0.7 0.6 %copy-done.5 = s32[1024]{0:T(1024)S(1)} copy-done((s32[1024]{0:T(1024)S(1)}, s32[1024]{0:T(1024)}, u32[]{:S(2)}) %copy-start.5) | copy-done | bytes 4120
  1.3 0.0 copy-done.6
  1.3 0.0 copy-done.7
  1.3 0.0 copy-done.8
  1.3 0.0 copy-start
  1.3 1.0 %copy-done = bf16[64,4096]{1,0:T(8,128)(2,1)S(1)} copy-done((bf16[64,4096]{1,0:T(8,128)(2,1)S(1)}, bf16[64,4096]{1,0:T(8,128)(2,1)}, u32[]{:S(2)}) %copy-start) | copy-done | bytes 524312
  2.4 0.0 copy-start.1
  2.4 0.9 %copy-done.1 = f32[30,16,16]{0,2,1:T(8,128)S(1)} copy-done((f32[30,16,16]{0,2,1:T(8,128)S(1)}, f32[30,16,16]{0,2,1:T(8,128)}, u32[]{:S(2)}) %copy-start.1) | copy-done | bytes 30744
  3.3 0.0 copy-start.2
  3.3 0.9 %copy-done.2 = f32[120,16,16]{0,2,1:T(8,128)S(1)} copy-done((f32[120,16,16]{0,2,1:T(8,128)S(1)}, f32[120,16,16]{0,2,1:T(8,128)}, u32[]{:S(2)}) %copy-start.2) | copy-done | bytes 122904
  4.2 0.0 copy-start.3
  4.2 0.8 %copy-done.3 = bf16[32,1024]{1,0:T(8,128)(2,1)S(1)} copy-done((bf16[32,1024]{1,0:T(8,128)(2,1)S(1)}, bf16[32,1024]{1,0:T(8,128)(2,1)}, u32[]{:S(2)}) %copy-start.3) | copy-done | bytes 65560
  5.0 0.0 copy-start.4
  5.0 0.8 %copy-done.4 = bf16[16,1024]{1,0:T(8,128)(2,1)S(1)} copy-done((bf16[16,1024]{1,0:T(8,128)(2,1)S(1)}, bf16[16,1024]{1,0:T(8,128)(2,1)}, u32[]{:S(2)}) %copy-start.4) | copy-done | bytes 32792
  5.8 37.0 %shard_map.120 = (bf16[32,1024]{1,0:T(8,128)(2,1)S(1)}, f32[1,16,32]{2,1,0:T(8,128)S(1)}, f32[1,16,16]{2,1,0:T(8,128)S(1)}, f32[1,16,16]{2,1,0:T(8,128)S(1)}) custom-call(bf16[32,1024]{1,0:T(8,128)(2,1)S(1)} %copy-done.3, s32[8,128]{1,0:T(8,128)S(1)} %bitcast.6, s32[64]{0:T(128)S(1)} %copy-done.6, s32[1,64]{1,0:T(1,128)S(1)} %bitcast.7, s32[64]{0:T(128)S(1)} %copy-done.7, ...), custom_call_target="tpu_custom_call" | custom-call | tf_op jit(solution)/shard_map/pallas_call | solution.py:378
  42.8 0.6 %copy.17 = bf16[32,1024]{1,0:T(8,128)(2,1)} copy(bf16[32,1024]{1,0:T(8,128)(2,1)S(1)} %get-tuple-element.8) | data formatting | bytes 131072
  43.5 0.6 %copy.18 = f32[1,16,32]{2,1,0:T(8,128)} copy(f32[1,16,32]{2,1,0:T(8,128)S(1)} %get-tuple-element.9) | data formatting | bytes 4096
  44.0 0.6 %copy.19 = f32[1,16,16]{2,1,0:T(8,128)} copy(f32[1,16,16]{2,1,0:T(8,128)S(1)} %get-tuple-element.10) | data formatting | bytes 2048
  44.6 0.6 %copy.20 = f32[1,16,16]{2,1,0:T(8,128)} copy(f32[1,16,16]{2,1,0:T(8,128)S(1)} %get-tuple-element.11) | data formatting | bytes 2048
Async XLA Ops:
  0.6 0.7 %copy-start.5 = (s32[1024]{0:T(1024)S(1)}, s32[1024]{0:T(1024)}, u32[]{:S(2)}) copy-start(s32[1024]{0:T(1024)} %param.10) | copy-start | bytes 12292
  0.6 0.7 %copy-start.6 = (s32[64]{0:T(128)S(1)}, s32[64]{0:T(128)}, u32[]{:S(2)}) copy-start(s32[64]{0:T(128)} %counts_ref.1) | copy-start | bytes 772
  0.7 0.7 %copy-start.7 = (s32[64]{0:T(128)S(1)}, s32[64]{0:T(128)}, u32[]{:S(2)}) copy-start(s32[64]{0:T(128)} %cols_ref.1) | copy-start | bytes 772
  0.7 0.7 %copy-start.8 = (f32[64]{0:T(128)S(1)}, f32[64]{0:T(128)}, u32[]{:S(2)}) copy-start(f32[64]{0:T(128)} %scales_ref.1) | copy-start | bytes 772
  1.3 1.0 %copy-start = (bf16[64,4096]{1,0:T(8,128)(2,1)S(1)}, bf16[64,4096]{1,0:T(8,128)(2,1)}, u32[]{:S(2)}) copy-start(bf16[64,4096]{1,0:T(8,128)(2,1)} %mats_hbm.1) | copy-start | bytes 1572868
  2.4 0.9 %copy-start.1 = (f32[30,16,16]{0,2,1:T(8,128)S(1)}, f32[30,16,16]{0,2,1:T(8,128)}, u32[]{:S(2)}) copy-start(f32[30,16,16]{0,2,1:T(8,128)} %param.16) | copy-start | bytes 92164
  3.3 0.9 %copy-start.2 = (f32[120,16,16]{0,2,1:T(8,128)S(1)}, f32[120,16,16]{0,2,1:T(8,128)}, u32[]{:S(2)}) copy-start(f32[120,16,16]{0,2,1:T(8,128)} %param.17) | copy-start | bytes 368644
  4.2 0.8 %copy-start.3 = (bf16[32,1024]{1,0:T(8,128)(2,1)S(1)}, bf16[32,1024]{1,0:T(8,128)(2,1)}, u32[]{:S(2)}) copy-start(bf16[32,1024]{1,0:T(8,128)(2,1)} %x_ref.1) | copy-start | bytes 196612
  5.0 0.8 %copy-start.4 = (bf16[16,1024]{1,0:T(8,128)(2,1)S(1)}, bf16[16,1024]{1,0:T(8,128)(2,1)}, u32[]{:S(2)}) copy-start(bf16[16,1024]{1,0:T(8,128)(2,1)} %bases_ref.1) | copy-start | bytes 98308

commit v2 on v1

--- a/solution.py
+++ b/solution.py
@@ -13,6 +13,7 @@
 REACH = 2
 CROSS = 4
 CAP = 32
+SIDE = 8
 LANES = 128
 MESH = pl.DeviceIdType.MESH
 HIGH = lax.Precision.HIGHEST
@@ -66,11 +67,12 @@
 
 
 def body(
-    devices, panels, x_ref, order_ref, counts_ref, countv_ref, cols_ref, scales_ref, mats_hbm,
-    bases_ref, local_hbm, cross_hbm, near_ref, coeffs_ref, factor_ref, topgram_ref,
-    mats, local_v, cross_v, sorted_ref, out, recv, own, ext, moment_out, moment_in, gram_out, gram_in,
+    devices, panels, x_hbm, order_hbm, counts_hbm, countv_hbm, cols_hbm, scales_hbm, mats_hbm,
+    bases_hbm, local_hbm, cross_hbm, near_ref, coeffs_ref, factor_ref, topgram_ref,
+    x_ref, order_ref, counts_ref, countv_ref, cols_ref, scales_ref, mats, bases_ref, local_v, cross_v,
+    sorted_ref, out, middle, recv, own, ext, moment_out, moment_in, gram_out, gram_in,
     top_out, top_in, hot_ref, quarter_ref,
-    mats_sem, local_sem, cross_sem, a2a_send, a2a_recv, gram_send, gram_recv, moment_send, moment_recv,
+    load_sems, one_send, one_recv, two_send, two_recv, gram_send, gram_recv, moment_send, moment_recv,
     top_send, top_recv, left_send, left_recv, right_send, right_recv,
 ):
     me = lax.axis_index("cluster")
@@ -81,31 +83,44 @@
     channels, points = x_ref.shape
     leaves = points // LEAF
 
-    load_mats = pltpu.make_async_copy(mats_hbm, mats, mats_sem)
-    load_local = pltpu.make_async_copy(local_hbm, local_v, local_sem)
-    load_cross = pltpu.make_async_copy(cross_hbm, cross_v, cross_sem)
-    load_local.start()
-    load_cross.start()
-    load_mats.start()
+    rows = devices // SIDE
+    y = lax.rem(me, SIDE)
+    z = me // SIDE
+    y_first = 1 - lax.rem(panel, 2)
+    z_first = 1 - y_first
+
+    def load(source, target, at):
+        copy = pltpu.make_async_copy(source, target, load_sems.at[at])
+        copy.start()
+        return copy
+
+    load_x = load(x_hbm, x_ref, 0)
+    load_order = load(order_hbm, order_ref, 1)
+    load_counts = load(counts_hbm, counts_ref, 2)
+    load_local = load(local_hbm, local_v, 3)
+    load_cross = load(cross_hbm, cross_v, 4)
+    load_bases = load(bases_hbm, bases_ref, 5)
+    load_countv = load(countv_hbm, countv_ref, 6)
+    load_cols = load(cols_hbm, cols_ref, 7)
+    load_scales = load(scales_hbm, scales_ref, 8)
+    load_mats = load(mats_hbm, mats, 9)
 
     barrier = pltpu.get_barrier_semaphore()
 
-    def greet(m, carry):
+    def at(dz, dy):
+        return lax.rem(z + dz, rows) * SIDE + lax.rem(y + dy, SIDE)
+
+    for k in range(1, SIDE):
+        pl.semaphore_signal(barrier, 1, device_id=(at(0, k), panel), device_id_type=MESH)
+    for k in range(1, rows):
+        pl.semaphore_signal(barrier, 1, device_id=(at(k, 0), panel), device_id_type=MESH)
+    for k in range(1, panels):
         pl.semaphore_signal(
-            barrier, 1, device_id=(lax.rem(me + m, devices), panel), device_id_type=MESH
+            barrier, 1, device_id=(me, lax.rem(panel + k, panels)), device_id_type=MESH
         )
-        return carry
-
-    lax.fori_loop(1, devices, greet, 0, unroll=9)
-
-    def greet_panel(m, carry):
-        pl.semaphore_signal(
-            barrier, 1, device_id=(me, lax.rem(panel + m, panels)), device_id_type=MESH
-        )
-        return carry
-
-    lax.fori_loop(1, panels, greet_panel, 0, unroll=7)
-
+
+    load_x.wait()
+    load_order.wait()
     x4 = jnp.concatenate([x_ref[...]] * 4, axis=0)
     point = iota((LANES, points), 1)
     hots = []
@@ -116,28 +131,34 @@
     sorted_ref[pl.ds(0, points), :] = dot_t(jnp.concatenate(hots, axis=0), x4)
     sorted_ref[pl.ds(points, CAP), :] = jnp.zeros((CAP, LANES), F32)
 
+    load_counts.wait()
     part = iota((8, LANES), 1) // channels
 
     def fill(m, start):
-        rows = [sorted_ref[pl.ds(start + 8 * q, 8), :] for q in range(4)]
-        low = jnp.where(part == 0, rows[0], rows[1])
-        high = jnp.where(part == 2, rows[2], rows[3])
-        out[m] = jnp.where(part < 2, low, high).astype(BF16)
+        cuts = [sorted_ref[pl.ds(start + 8 * q, 8), :] for q in range(4)]
+        low = jnp.where(part == 0, cuts[0], cuts[1])
+        high = jnp.where(part == 2, cuts[2], cuts[3])
+        dy = lax.rem(m, SIDE)
+        dz = lax.rem(m // SIDE + (y + dy) // SIDE, rows)
+        out[y_first * dy + z_first * dz, y_first * dz + z_first * dy] = jnp.where(
+            part < 2, low, high
+        ).astype(BF16)
         return start + counts_ref[m]
 
     lax.fori_loop(0, devices, fill, 0, unroll=8)
 
-    pl.semaphore_wait(barrier, devices - 1 + panels - 1)
-
-    def send(m, carry):
+    pl.semaphore_wait(barrier, SIDE - 1 + rows - 1 + panels - 1)
+
+    one = [
         pltpu.make_async_remote_copy(
-            out.at[m], recv.at[m], a2a_send, a2a_recv,
-            device_id=(lax.rem(me + m, devices), panel), device_id_type=MESH,
-        ).start()
-        return carry
-
-    lax.fori_loop(1, devices, send, 0, unroll=9)
-    recv[0] = out[0]
+            out.at[k], middle.at[k], one_send, one_recv,
+            device_id=(at(z_first * k, y_first * k), panel), device_id_type=MESH,
+        )
+        for k in range(1, SIDE)
+    ]
+    for copy in one:
+        copy.start()
+    middle[0] = out[0]
 
     load_local.wait()
     load_cross.wait()
@@ -185,6 +206,7 @@
     spread = iota((LANES, points), 0)
     spread = ((spread % leaves == iota((LANES, points), 1) // LEAF) & (spread < 3 * leaves))
     path = dot(terms, spread.astype(F32).astype(BF16)).reshape(RANK, RANK, points)
+    load_bases.wait()
     bases = bases_ref[...].astype(F32)
     weights = path[0] * bases[0:1]
     for k in range(1, RANK):
@@ -200,15 +222,7 @@
     gram_out[...] = packed
     gram_in[rank_in] = packed
 
-    def send_gram(m, carry):
-        pltpu.make_async_remote_copy(
-            gram_out, gram_in.at[rank_in], gram_send, gram_recv,
-            device_id=(base + lax.rem(rank_in + m, group), panel), device_id_type=MESH,
-        ).start()
-        return carry
-
-    lax.fori_loop(1, group, send_gram, 0, unroll=15)
-
+    load_countv.wait()
     counts = countv_ref[...].astype(F32)
     square = (devices, devices)
     upto = (iota(square, 0) <= iota(square, 1)).astype(F32).astype(BF16)
@@ -221,7 +235,9 @@
     within = (iota((points, LANES), 0).astype(F32) - passed[:, :LANES]).astype(jnp.int32)
     run = passed[:, LANES:].astype(jnp.int32)
     quarter_ref[...] = (within // 8 == iota((points, LANES), 1) // channels).astype(F32)
-    slot = run * 8 + within % 8
+    dy = run % SIDE
+    dz = (run // SIDE + (dy > y).astype(jnp.int32)) % rows
+    slot = (y_first * (dz * SIDE + dy) + z_first * (dy * rows + dz)) * 8 + within % 8
     slots = devices * 8
     hot_ref[...] = (
         (jnp.concatenate([slot] * (slots // LANES), axis=1) == iota((points, slots), 1))
@@ -229,8 +245,29 @@
         .astype(BF16)
     )
 
-    others = pl.ds(1, devices - 1)
-    pltpu.make_async_copy(recv.at[others], recv.at[others], a2a_recv).wait()
+    others = pl.ds(1, SIDE - 1)
+    pltpu.make_async_copy(middle.at[others], middle.at[others], one_recv).wait()
+    two = [
+        pltpu.make_async_remote_copy(
+            middle.at[:, k], recv.at[k], two_send, two_recv,
+            device_id=(at(y_first * k, z_first * k), panel), device_id_type=MESH,
+        )
+        for k in range(1, SIDE)
+    ]
+    for copy in two:
+        copy.start()
+    recv[0] = middle[:, 0]
+
+    def send_gram(m, carry):
+        pltpu.make_async_remote_copy(
+            gram_out, gram_in.at[rank_in], gram_send, gram_recv,
+            device_id=(base + lax.rem(rank_in + m, group), panel), device_id_type=MESH,
+        ).start()
+        return carry
+
+    lax.fori_loop(1, group, send_gram, 0, unroll=15)
+
+    pltpu.make_async_copy(recv.at[others], recv.at[others], two_recv).wait()
 
     received = recv[...].astype(F32).reshape(slots, LANES).astype(BF16)
     relaid = dot(hot_ref[...], received)
@@ -288,6 +325,8 @@
     factor_ref[0] = jnp.where(lane >= sub, tableau, 0.0)[:, :RANK]
     inverse = tableau[:, RANK : 2 * RANK]
 
+    load_cols.wait()
+    load_scales.wait()
     load_mats.wait()
 
     def near_leaf(i, source, first):
@@ -350,7 +389,8 @@
     pltpu.make_async_copy(top_in.at[peers], top_in.at[peers], top_recv).wait()
     topgram_ref[0] = unpack2(jnp.sum(top_in[...], axis=0))[:, :RANK]
 
-    pltpu.make_async_copy(out.at[others], out.at[others], a2a_send).wait()
+    pltpu.make_async_copy(out.at[others], out.at[others], one_send).wait()
+    pltpu.make_async_copy(recv.at[others], recv.at[others], two_send).wait()
     peers = pl.ds(0, group - 1)
     pltpu.make_async_copy(gram_in.at[peers], gram_in.at[peers], gram_send).wait()
     pltpu.make_async_copy(moment_in.at[peers], moment_in.at[peers], moment_send).wait()
@@ -370,28 +410,40 @@
     leaves = points // LEAF
     group = 2**CROSS
     vmem = pl.BlockSpec(memory_space=pltpu.VMEM)
-    smem = pl.BlockSpec(memory_space=pltpu.SMEM)
     hbm = pl.BlockSpec(memory_space=pl.ANY)
-    local_t = jnp.transpose(local_tiles, (1, 2, 0))
-    cross_t = jnp.transpose(cross_tiles, (1, 2, 0))
     dma = pltpu.SemaphoreType.DMA
-    return pl.pallas_call(
+    operands = (
+        inputs,
+        local_order.reshape(points // LANES, LANES),
+        run_counts,
+        run_counts.reshape(1, devices),
+        near_cols,
+        near_scales,
+        near_blocks,
+        leaf_bases,
+        jnp.transpose(local_tiles, (1, 2, 0)),
+        jnp.transpose(cross_tiles, (1, 2, 0)),
+    )
+    operands = [pltpu.with_memory_space_constraint(x, pltpu.HBM) for x in operands]
+    spaces = [pltpu.VMEM, pltpu.VMEM, pltpu.SMEM, pltpu.VMEM, pltpu.SMEM, pltpu.SMEM] + [pltpu.VMEM] * 4
+    slots = (SIDE, SIDE, 8, LANES)
+    shapes = (
+        ((channels, points), BF16),
+        ((1, RANK, channels), F32),
+        ((1, RANK, RANK), F32),
+        ((1, RANK, RANK), F32),
+    )
+    results = pl.pallas_call(
         functools.partial(body, devices, panels),
-        out_shape=(
-            jax.ShapeDtypeStruct((channels, points), BF16),
-            jax.ShapeDtypeStruct((1, RANK, channels), F32),
-            jax.ShapeDtypeStruct((1, RANK, RANK), F32),
-            jax.ShapeDtypeStruct((1, RANK, RANK), F32),
-        ),
-        in_specs=[vmem, vmem, smem, vmem, smem, smem, hbm, vmem, hbm, hbm],
-        out_specs=(vmem, vmem, vmem, vmem),
-        scratch_shapes=[
-            pltpu.VMEM(near_blocks.shape, BF16),
-            pltpu.VMEM(local_t.shape, F32),
-            pltpu.VMEM(cross_t.shape, F32),
+        out_shape=tuple(pltpu.VMEM(*s) for s in shapes),
+        in_specs=[hbm] * len(operands),
+        out_specs=(vmem,) * 4,
+        scratch_shapes=[space(x.shape, x.dtype) for space, x in zip(spaces, operands)]
+        + [
             pltpu.VMEM((points + CAP, LANES), F32),
-            pltpu.VMEM((devices, 8, LANES), BF16),
-            pltpu.VMEM((devices, 8, LANES), BF16),
+            pltpu.VMEM(slots, BF16),
+            pltpu.VMEM(slots, BF16),
+            pltpu.VMEM(slots, BF16),
             pltpu.VMEM((leaves, channels, LEAF), BF16),
             pltpu.VMEM((leaves + 2 * REACH, channels, LEAF), BF16),
             pltpu.VMEM((4, LANES), F32),
@@ -402,23 +454,29 @@
             pltpu.VMEM((panels, 2, LANES), F32),
             pltpu.VMEM((points, devices * 8), BF16),
             pltpu.VMEM((points, LANES), F32),
+            dma((len(operands),)),
         ]
-        + [dma] * 15,
+        + [dma] * 14,
         compiler_params=pltpu.CompilerParams(
             collective_id=0, has_side_effects=True, vmem_limit_bytes=48 * 2**20
         ),
-    )(
-        inputs,
-        local_order.reshape(points // LANES, LANES),
-        run_counts,
-        run_counts.reshape(1, devices),
-        near_cols,
-        near_scales,
-        near_blocks,
-        leaf_bases,
-        local_t,
-        cross_t,
-    )
+    )(*operands)
+    return pl.pallas_call(
+        store,
+        out_shape=tuple(jax.ShapeDtypeStruct(*s) for s in shapes),
+        in_specs=[hbm] * 4,
+        out_specs=(hbm,) * 4,
+        scratch_shapes=[dma((4,))],
+    )(*[pltpu.with_memory_space_constraint(x, pltpu.VMEM) for x in results])
+
+
+def store(*refs):
+    sems = refs[8]
+    copies = [pltpu.make_async_copy(refs[k], refs[4 + k], sems.at[k]) for k in range(4)]
+    for copy in copies:
+        copy.start()
+    for copy in copies:
+        copy.wait()
 
 
 def solution(mesh):

time: 45.6 us -> 38.6 us (0.85)
  local copies, waits for them, and re-layouts: 7.54 us -> 0 us
  Pallas kernels: 37 us -> 37.8 us
    unnamed x22 -> x0, local copies, waits for them, and re-layouts: 7.54 us -> none
    pallas_call x1 -> x2, Pallas kernels: 37 us -> 37.8 us  [the longest x1 37.2 us: on_device(): pl.pallas_call(functools.partial(body, devices, panels), out_shape=tuple(...]
where the time goes in v2:
time: 38.6 us; the launch traced here: 38.5 us
  Pallas kernels  37.8 us (98%)
  between operations  0.64 us (2%)
    pallas_call x1, Pallas kernels, on_device(): pl.pallas_call(functools.partial(body, devices, panels), out_shape=tuple(...  37.2 us

profile of v2, /device:TPU:1, one launch (start us, length us, event | category | flops | bytes accessed | tf_op | source)
XLA Modules:
  0.0 38.5 jit_solution(10738921769379368090)
XLA Ops:
  0.6 37.2 %shard_map.120 = (bf16[32,1024]{1,0:T(8,128)(2,1)S(1)}, f32[1,16,32]{2,1,0:T(8,128)S(1)}, f32[1,16,16]{2,1,0:T(8,128)S(1)}, f32[1,16,16]{2,1,0:T(8,128)S(1)}) custom-call(bf16[32,1024]{1,0:T(8,128)(2,1)} %x_hbm.1, s32[8,128]{1,0:T(8,128)} %bitcast.6, s32[64]{0:T(128)} %counts_hbm.1, s32[1,64]{1,0:T(1,128)} %bitcast.7, s32[64]{0:T(128)} %cols_hbm.1, ...), custom_call_target="tpu_custom_call" | custom-call | tf_op jit(solution)/shard_map/pallas_call | solution.py:436
  37.8 0.7 %shard_map.121 = (bf16[32,1024]{1,0:T(8,128)(2,1)}, f32[1,16,32]{2,1,0:T(8,128)}, f32[1,16,16]{2,1,0:T(8,128)}, f32[1,16,16]{2,1,0:T(8,128)}) custom-call(bf16[32,1024]{1,0:T(8,128)(2,1)S(1)} %get-tuple-element.8.refs_0_, f32[1,16,32]{2,1,0:T(8,128)S(1)} %get-tuple-element.9.refs_1_, f32[1,16,16]{2,1,0:T(8,128)S(1)} %get-tuple-element.10.refs_2_, ...), custom_call_target="tpu_custom_call" | custom-call | tf_op jit(solution)/shard_map/pallas_call | solution.py:464

commit v3 on v2

--- a/solution.py
+++ b/solution.py
@@ -70,9 +70,9 @@
     devices, panels, x_hbm, order_hbm, counts_hbm, countv_hbm, cols_hbm, scales_hbm, mats_hbm,
     bases_hbm, local_hbm, cross_hbm, near_ref, coeffs_ref, factor_ref, topgram_ref,
     x_ref, order_ref, counts_ref, countv_ref, cols_ref, scales_ref, mats, bases_ref, local_v, cross_v,
-    sorted_ref, out, middle, recv, own, ext, moment_out, moment_in, gram_out, gram_in,
+    sorted_ref, out, middle, recv, weight_out, weight_in, own, ext, moment_out, moment_in, gram_out, gram_in,
     top_out, top_in, hot_ref, quarter_ref,
-    load_sems, one_send, one_recv, two_send, two_recv, gram_send, gram_recv, moment_send, moment_recv,
+    load_sems, one_send, one_recv, weight_send, weight_recv, two_send, two_recv, gram_send, gram_recv, moment_send, moment_recv,
     top_send, top_recv, left_send, left_recv, right_send, right_recv,
 ):
     me = lax.axis_index("cluster")
@@ -86,8 +86,6 @@
     rows = devices // SIDE
     y = lax.rem(me, SIDE)
     z = me // SIDE
-    y_first = 1 - lax.rem(panel, 2)
-    z_first = 1 - y_first
 
     def load(source, target, at):
         copy = pltpu.make_async_copy(source, target, load_sems.at[at])
@@ -114,6 +112,9 @@
         pl.semaphore_signal(barrier, 1, device_id=(at(0, k), panel), device_id_type=MESH)
     for k in range(1, rows):
         pl.semaphore_signal(barrier, 1, device_id=(at(k, 0), panel), device_id_type=MESH)
+    twin = 1 - 2 * lax.rem(z, 2) + rows
+    for k in range(1, SIDE):
+        pl.semaphore_signal(barrier, 1, device_id=(at(twin, k), panel), device_id_type=MESH)
     for k in range(1, panels):
         pl.semaphore_signal(
             barrier, 1, device_id=(me, lax.rem(panel + k, panels)), device_id_type=MESH
@@ -140,25 +141,10 @@
         high = jnp.where(part == 2, cuts[2], cuts[3])
         dy = lax.rem(m, SIDE)
         dz = lax.rem(m // SIDE + (y + dy) // SIDE, rows)
-        out[y_first * dy + z_first * dz, y_first * dz + z_first * dy] = jnp.where(
-            part < 2, low, high
-        ).astype(BF16)
+        out[dz, dy] = jnp.where(part < 2, low, high).astype(BF16)
         return start + counts_ref[m]
 
     lax.fori_loop(0, devices, fill, 0, unroll=8)
-
-    pl.semaphore_wait(barrier, SIDE - 1 + rows - 1 + panels - 1)
-
-    one = [
-        pltpu.make_async_remote_copy(
-            out.at[k], middle.at[k], one_send, one_recv,
-            device_id=(at(z_first * k, y_first * k), panel), device_id_type=MESH,
-        )
-        for k in range(1, SIDE)
-    ]
-    for copy in one:
-        copy.start()
-    middle[0] = out[0]
 
     load_local.wait()
     load_cross.wait()
@@ -222,6 +208,27 @@
     gram_out[...] = packed
     gram_in[rank_in] = packed
 
+    pl.semaphore_wait(barrier, 2 * (SIDE - 1) + rows - 1 + panels - 1)
+
+    one = [
+        pltpu.make_async_remote_copy(
+            out.at[k], middle.at[k], one_send, one_recv,
+            device_id=(at(k, 0), panel), device_id_type=MESH,
+        )
+        for k in range(1, rows)
+    ]
+    for copy in one:
+        copy.start()
+    middle[0] = out[0]
+    def send_gram(m, carry):
+        pltpu.make_async_remote_copy(
+            gram_out, gram_in.at[rank_in], gram_send, gram_recv,
+            device_id=(base + lax.rem(rank_in + m, group), panel), device_id_type=MESH,
+        ).start()
+        return carry
+
+    lax.fori_loop(1, group, send_gram, 0, unroll=15)
+
     load_countv.wait()
     counts = countv_ref[...].astype(F32)
     square = (devices, devices)
@@ -237,7 +244,7 @@
     quarter_ref[...] = (within // 8 == iota((points, LANES), 1) // channels).astype(F32)
     dy = run % SIDE
     dz = (run // SIDE + (dy > y).astype(jnp.int32)) % rows
-    slot = (y_first * (dz * SIDE + dy) + z_first * (dy * rows + dz)) * 8 + within % 8
+    slot = (dy * rows + dz) * 8 + within % 8
     slots = devices * 8
     hot_ref[...] = (
         (jnp.concatenate([slot] * (slots // LANES), axis=1) == iota((points, slots), 1))
@@ -245,12 +252,64 @@
         .astype(BF16)
     )
 
+    lower = (iota(square, 1) <= iota(square, 0)).astype(F32).astype(BF16)
+    ends_col = dot(lower, counts_col.astype(BF16))
+    passed_row = (
+        (jnp.concatenate([ends_col] * (points // LANES), axis=1) <= iota((devices, points), 1).astype(F32))
+        .astype(F32)
+        .astype(BF16)
+    )
+    starts_row = dot(jnp.broadcast_to(counts, (8, devices)).astype(BF16), passed_row)[0:1]
+    quarter_row = (iota((1, points), 1).astype(F32) - starts_row).astype(jnp.int32) // 8
+    pair = jnp.concatenate([parts[0], parts[1]], axis=0).astype(F32)
+    keep = quarter_row == iota((4 * 2 * RANK, points), 0) // (2 * RANK)
+    spaced = jnp.where(keep, jnp.concatenate([pair] * 4, axis=0), 0.0).astype(BF16)
+    spaced = dot(spaced, hot_ref[...]).T.astype(BF16)
+    weight_out[...] = spaced.reshape(SIDE, slots // SIDE, LANES)
+
+    for k in range(1, SIDE):
+        pltpu.make_async_remote_copy(
+            weight_out.at[k], weight_in.at[k], weight_send, weight_recv,
+            device_id=(at(0, SIDE - k), panel), device_id_type=MESH,
+        ).start()
+    weight_in[0] = weight_out[0]
+
     others = pl.ds(1, SIDE - 1)
+    pltpu.make_async_copy(weight_in.at[others], weight_in.at[others], weight_recv).wait()
     pltpu.make_async_copy(middle.at[others], middle.at[others], one_recv).wait()
+
+    held = jnp.concatenate(
+        [middle[:, k].astype(F32).reshape(rows * 8, LANES) for k in range(SIDE)], axis=0
+    ).astype(BF16)
+    moment = lax.dot_general(
+        weight_in[...].reshape(slots, LANES), held, (((0,), (0,)), ((), ())),
+        preferred_element_type=F32,
+    )
+    part = iota((2 * RANK, LANES), 1) // channels
+    moment = sum(
+        jnp.where(part == q, moment[q * 2 * RANK : (q + 1) * 2 * RANK], 0.0) for q in range(4)
+    )
+    moment = group_sum(moment[:RANK] + moment[RANK:], channels)
+    part = iota((4, LANES), 1) // channels
+    low = jnp.where(part == 0, moment[0:4], moment[4:8])
+    high = jnp.where(part == 2, moment[8:12], moment[12:16])
+    packed = jnp.where(part < 2, low, high)
+    moment_out[...] = packed
+    moment_in[rank_in] = packed
+
+    def send_moment(m, carry):
+        pltpu.make_async_remote_copy(
+            moment_out, moment_in.at[rank_in], moment_send, moment_recv,
+            device_id=(base + lax.rem(rank_in + m, group), panel), device_id_type=MESH,
+        ).start()
+        return carry
+
+    lax.fori_loop(1, group, send_moment, 0, unroll=15)
+
     two = [
         pltpu.make_async_remote_copy(
             middle.at[:, k], recv.at[k], two_send, two_recv,
-            device_id=(at(y_first * k, z_first * k), panel), device_id_type=MESH,
+            device_id=(at(0, k), panel), device_id_type=MESH,
         )
         for k in range(1, SIDE)
     ]
@@ -258,39 +317,46 @@
         copy.start()
     recv[0] = middle[:, 0]
 
-    def send_gram(m, carry):
+    peers = pl.ds(0, group - 1)
+    pltpu.make_async_copy(gram_in.at[peers], gram_in.at[peers], gram_recv).wait()
+    sub = iota((RANK, LANES), 0)
+    lane = iota((RANK, LANES), 1)
+    tableau = jnp.where(
+        lane < RANK, unpack2(jnp.sum(gram_in[...], axis=0)), (lane - RANK == sub).astype(F32)
+    )
+    for k in range(RANK - 1):
+        ratio = tableau[:, k : k + 1] / tableau[k : k + 1, k : k + 1]
+        tableau = tableau - jnp.where(sub > k, ratio * tableau[k : k + 1, :], 0.0)
+    pivots = jnp.sum(jnp.where(lane == sub, tableau, 0.0), axis=1, keepdims=True)
+    tableau = tableau * (1.0 / jnp.sqrt(pivots))
+    factor_ref[0] = jnp.where(lane >= sub, tableau, 0.0)[:, :RANK]
+    inverse = tableau[:, RANK : 2 * RANK]
+
+    pltpu.make_async_copy(moment_in.at[peers], moment_in.at[peers], moment_recv).wait()
+    packed = jnp.sum(moment_in[...], axis=0)
+    moment = jnp.concatenate(
+        [packed[:, q * channels : (q + 1) * channels] for q in range(4)], axis=0
+    )
+    coeffs = dot(inverse, moment, HIGH)
+    coeffs_ref[0] = coeffs
+    packed = pack2(dot_t(coeffs, jnp.concatenate([coeffs] * 8, axis=0), HIGH))
+    top_out[...] = packed
+    top_in[panel] = packed
+
+    def send_top(m, carry):
         pltpu.make_async_remote_copy(
-            gram_out, gram_in.at[rank_in], gram_send, gram_recv,
-            device_id=(base + lax.rem(rank_in + m, group), panel), device_id_type=MESH,
+            top_out, top_in.at[panel], top_send, top_recv,
+            device_id=(me, lax.rem(panel + m, panels)), device_id_type=MESH,
         ).start()
         return carry
 
-    lax.fori_loop(1, group, send_gram, 0, unroll=15)
+    lax.fori_loop(1, panels, send_top, 0, unroll=7)
 
     pltpu.make_async_copy(recv.at[others], recv.at[others], two_recv).wait()
 
     received = recv[...].astype(F32).reshape(slots, LANES).astype(BF16)
     relaid = dot(hot_ref[...], received)
     relaid = jnp.where(quarter_ref[...] > 0.5, relaid, 0.0).astype(BF16)
-
-    moment = dot(weights3, relaid)
-    moment = moment[0:RANK] + moment[RANK : 2 * RANK] + moment[2 * RANK :]
-    moment = group_sum(moment, channels)
-    part = iota((4, LANES), 1) // channels
-    low = jnp.where(part == 0, moment[0:4], moment[4:8])
-    high = jnp.where(part == 2, moment[8:12], moment[12:16])
-    packed = jnp.where(part < 2, low, high)
-    moment_out[...] = packed
-    moment_in[rank_in] = packed
-
-    def send_moment(m, carry):
-        pltpu.make_async_remote_copy(
-            moment_out, moment_in.at[rank_in], moment_send, moment_recv,
-            device_id=(base + lax.rem(rank_in + m, group), panel), device_id_type=MESH,
-        ).start()
-        return carry
-
-    lax.fori_loop(1, group, send_moment, 0, unroll=15)
 
     fold = (iota((channels, LANES), 1) % channels == iota((channels, LANES), 0)).astype(F32).astype(BF16)
     for n in range(leaves):
@@ -307,23 +373,25 @@
         own.at[pl.ds(leaves - REACH, REACH)], ext.at[pl.ds(0, REACH)], right_send, right_recv,
         device_id=(right, panel), device_id_type=MESH,
     )
-    to_left.start()
-    to_right.start()
-
-    peers = pl.ds(0, group - 1)
-    pltpu.make_async_copy(gram_in.at[peers], gram_in.at[peers], gram_recv).wait()
-    sub = iota((RANK, LANES), 0)
-    lane = iota((RANK, LANES), 1)
-    tableau = jnp.where(
-        lane < RANK, unpack2(jnp.sum(gram_in[...], axis=0)), (lane - RANK == sub).astype(F32)
-    )
-    for k in range(RANK - 1):
-        ratio = tableau[:, k : k + 1] / tableau[k : k + 1, k : k + 1]
-        tableau = tableau - jnp.where(sub > k, ratio * tableau[k : k + 1, :], 0.0)
-    pivots = jnp.sum(jnp.where(lane == sub, tableau, 0.0), axis=1, keepdims=True)
-    tableau = tableau * (1.0 / jnp.sqrt(pivots))
-    factor_ref[0] = jnp.where(lane >= sub, tableau, 0.0)[:, :RANK]
-    inverse = tableau[:, RANK : 2 * RANK]
+    has_left = me > 0
+    has_right = me < devices - 1
+
+    @pl.when(has_left)
+    def _():
+        to_left.start()
+
+    @pl.when(has_right)
+    def _():
+        to_right.start()
+
+    @pl.when(me == 0)
+    def _():
+        ext[pl.ds(0, REACH)] = jnp.zeros((REACH, channels, LEAF), BF16)
+
+    @pl.when(me == devices - 1)
+    def _():
+        ext[pl.ds(leaves + REACH, REACH)] = jnp.zeros((REACH, channels, LEAF), BF16)
+
 
     load_cols.wait()
     load_scales.wait()
@@ -359,28 +427,14 @@
     for i in range(REACH, leaves - REACH, 2):
         near_pair(i, own, me * leaves)
 
-    pltpu.make_async_copy(moment_in.at[peers], moment_in.at[peers], moment_recv).wait()
-    packed = jnp.sum(moment_in[...], axis=0)
-    moment = jnp.concatenate(
-        [packed[:, q * channels : (q + 1) * channels] for q in range(4)], axis=0
-    )
-    coeffs = dot(inverse, moment, HIGH)
-    coeffs_ref[0] = coeffs
-    packed = pack2(dot_t(coeffs, jnp.concatenate([coeffs] * 8, axis=0), HIGH))
-    top_out[...] = packed
-    top_in[panel] = packed
-
-    def send_top(m, carry):
-        pltpu.make_async_remote_copy(
-            top_out, top_in.at[panel], top_send, top_recv,
-            device_id=(me, lax.rem(panel + m, panels)), device_id_type=MESH,
-        ).start()
-        return carry
-
-    lax.fori_loop(1, panels, send_top, 0, unroll=7)
-
-    to_left.wait_recv()
-    to_right.wait_recv()
+    @pl.when(has_right)
+    def _():
+        to_left.wait_recv()
+
+    @pl.when(has_left)
+    def _():
+        to_right.wait_recv()
+
     first = me * leaves - REACH
     near_pair(0, ext, first)
     near_pair(leaves - 2, ext, first)
@@ -390,14 +444,20 @@
     topgram_ref[0] = unpack2(jnp.sum(top_in[...], axis=0))[:, :RANK]
 
     pltpu.make_async_copy(out.at[others], out.at[others], one_send).wait()
+    pltpu.make_async_copy(weight_in.at[others], weight_in.at[others], weight_send).wait()
     pltpu.make_async_copy(recv.at[others], recv.at[others], two_send).wait()
     peers = pl.ds(0, group - 1)
     pltpu.make_async_copy(gram_in.at[peers], gram_in.at[peers], gram_send).wait()
     pltpu.make_async_copy(moment_in.at[peers], moment_in.at[peers], moment_send).wait()
     peers = pl.ds(0, panels - 1)
     pltpu.make_async_copy(top_in.at[peers], top_in.at[peers], top_send).wait()
-    to_left.wait_send()
-    to_right.wait_send()
+    @pl.when(has_left)
+    def _():
+        to_left.wait_send()
+
+    @pl.when(has_right)
+    def _():
+        to_right.wait_send()
 
 
 def on_device(
@@ -444,6 +504,8 @@
             pltpu.VMEM(slots, BF16),
             pltpu.VMEM(slots, BF16),
             pltpu.VMEM(slots, BF16),
+            pltpu.VMEM((SIDE, devices * 8 // SIDE, LANES), BF16),
+            pltpu.VMEM((SIDE, devices * 8 // SIDE, LANES), BF16),
             pltpu.VMEM((leaves, channels, LEAF), BF16),
             pltpu.VMEM((leaves + 2 * REACH, channels, LEAF), BF16),
             pltpu.VMEM((4, LANES), F32),
@@ -456,7 +518,7 @@
             pltpu.VMEM((points, LANES), F32),
             dma((len(operands),)),
         ]
-        + [dma] * 14,
+        + [dma] * 16,
         compiler_params=pltpu.CompilerParams(
             collective_id=0, has_side_effects=True, vmem_limit_bytes=48 * 2**20
         ),

time: 38.6 us -> 34.9 us (0.904)
  Pallas kernels: 37.8 us -> 34.2 us
    pallas_call x1, Pallas kernels: 37.2 us -> 33.5 us  [on_device(): pl.pallas_call(functools.partial(body, devices, panels), out_shape=tuple(...]
where the time goes in v3:
time: 34.9 us; the launch traced here: 34.8 us
  Pallas kernels  34.2 us (98%)
  between operations  0.64 us (2%)
    pallas_call x1, Pallas kernels, on_device(): pl.pallas_call(functools.partial(body, devices, panels), out_shape=tuple(...  33.5 us

profile of v3, /device:TPU:1, one launch (start us, length us, event | category | flops | bytes accessed | tf_op | source)
XLA Modules:
  0.0 34.8 jit_solution(11530663394798134905)
XLA Ops:
  0.6 33.5 %shard_map.120 = (bf16[32,1024]{1,0:T(8,128)(2,1)S(1)}, f32[1,16,32]{2,1,0:T(8,128)S(1)}, f32[1,16,16]{2,1,0:T(8,128)S(1)}, f32[1,16,16]{2,1,0:T(8,128)S(1)}) custom-call(bf16[32,1024]{1,0:T(8,128)(2,1)} %x_hbm.1, s32[8,128]{1,0:T(8,128)} %bitcast.6, s32[64]{0:T(128)} %counts_hbm.1, s32[1,64]{1,0:T(1,128)} %bitcast.7, s32[64]{0:T(128)} %cols_hbm.1, ...), custom_call_target="tpu_custom_call" | custom-call | tf_op jit(solution)/shard_map/pallas_call | solution.py:496
  34.1 0.7 %shard_map.121 = (bf16[32,1024]{1,0:T(8,128)(2,1)}, f32[1,16,32]{2,1,0:T(8,128)}, f32[1,16,16]{2,1,0:T(8,128)}, f32[1,16,16]{2,1,0:T(8,128)}) custom-call(bf16[32,1024]{1,0:T(8,128)(2,1)S(1)} %get-tuple-element.8.refs_0_, f32[1,16,32]{2,1,0:T(8,128)S(1)} %get-tuple-element.9.refs_1_, f32[1,16,16]{2,1,0:T(8,128)S(1)} %get-tuple-element.10.refs_2_, ...), custom_call_target="tpu_custom_call" | custom-call | tf_op jit(solution)/shard_map/pallas_call | solution.py:526

commit v4 on v3

--- a/solution.py
+++ b/solution.py
@@ -79,7 +79,6 @@
     panel = lax.axis_index("panel")
     group = 2**CROSS
     rank_in = lax.rem(me, group)
-    base = me - rank_in
     channels, points = x_ref.shape
     leaves = points // LEAF
 
@@ -108,13 +107,15 @@
     def at(dz, dy):
         return lax.rem(z + dz, rows) * SIDE + lax.rem(y + dy, SIDE)
 
-    for k in range(1, SIDE):
+    far = sorted(range(1, SIDE), key=lambda k: -min(k, SIDE - k))
+    for k in far:
+        pl.semaphore_signal(barrier, 1, device_id=(at(k, 0), panel), device_id_type=MESH)
+    for k in far:
         pl.semaphore_signal(barrier, 1, device_id=(at(0, k), panel), device_id_type=MESH)
-    for k in range(1, rows):
-        pl.semaphore_signal(barrier, 1, device_id=(at(k, 0), panel), device_id_type=MESH)
     twin = 1 - 2 * lax.rem(z, 2) + rows
     for k in range(1, SIDE):
         pl.semaphore_signal(barrier, 1, device_id=(at(twin, k), panel), device_id_type=MESH)
+    mates = [at(dz, k) for k in far for dz in (twin, 0)] + [at(twin, 0)]
     for k in range(1, panels):
         pl.semaphore_signal(
             barrier, 1, device_id=(me, lax.rem(panel + k, panels)), device_id_type=MESH
@@ -200,14 +201,6 @@
     parts = split3(weights)
     weights3 = jnp.concatenate(parts, axis=0)
 
-    wide = jnp.concatenate([p for p in parts for _ in range(8)], axis=0)
-    gram = dot_t(weights3, wide)
-    gram = gram[0:RANK] + gram[RANK : 2 * RANK] + gram[2 * RANK :]
-    gram = gram[:, 0:LANES] + gram[:, LANES : 2 * LANES] + gram[:, 2 * LANES :]
-    packed = pack2(gram)
-    gram_out[...] = packed
-    gram_in[rank_in] = packed
-
     pl.semaphore_wait(barrier, 2 * (SIDE - 1) + rows - 1 + panels - 1)
 
     one = [
@@ -215,20 +208,11 @@
             out.at[k], middle.at[k], one_send, one_recv,
             device_id=(at(k, 0), panel), device_id_type=MESH,
         )
-        for k in range(1, rows)
+        for k in far
     ]
     for copy in one:
         copy.start()
     middle[0] = out[0]
-    def send_gram(m, carry):
-        pltpu.make_async_remote_copy(
-            gram_out, gram_in.at[rank_in], gram_send, gram_recv,
-            device_id=(base + lax.rem(rank_in + m, group), panel), device_id_type=MESH,
-        ).start()
-        return carry
-
-    lax.fori_loop(1, group, send_gram, 0, unroll=15)
-
     load_countv.wait()
     counts = countv_ref[...].astype(F32)
     square = (devices, devices)
@@ -241,7 +225,6 @@
     passed = dot((ends <= position).astype(F32).astype(BF16), both)
     within = (iota((points, LANES), 0).astype(F32) - passed[:, :LANES]).astype(jnp.int32)
     run = passed[:, LANES:].astype(jnp.int32)
-    quarter_ref[...] = (within // 8 == iota((points, LANES), 1) // channels).astype(F32)
     dy = run % SIDE
     dz = (run // SIDE + (dy > y).astype(jnp.int32)) % rows
     slot = (dy * rows + dz) * 8 + within % 8
@@ -267,24 +250,38 @@
     spaced = dot(spaced, hot_ref[...]).T.astype(BF16)
     weight_out[...] = spaced.reshape(SIDE, slots // SIDE, LANES)
 
-    for k in range(1, SIDE):
+    for k in far:
         pltpu.make_async_remote_copy(
             weight_out.at[k], weight_in.at[k], weight_send, weight_recv,
             device_id=(at(0, SIDE - k), panel), device_id_type=MESH,
         ).start()
     weight_in[0] = weight_out[0]
 
+    wide = jnp.concatenate([p for p in parts for _ in range(8)], axis=0)
+    gram = dot_t(weights3, wide)
+    gram = gram[0:RANK] + gram[RANK : 2 * RANK] + gram[2 * RANK :]
+    gram = gram[:, 0:LANES] + gram[:, LANES : 2 * LANES] + gram[:, 2 * LANES :]
+    packed = pack2(gram)
+    gram_out[...] = packed
+    gram_in[rank_in] = packed
+
+    for peer in mates:
+        pltpu.make_async_remote_copy(
+            gram_out, gram_in.at[rank_in], gram_send, gram_recv,
+            device_id=(peer, panel), device_id_type=MESH,
+        ).start()
+
+    quarter_ref[...] = (within // 8 == iota((points, LANES), 1) // channels).astype(F32)
+
     others = pl.ds(1, SIDE - 1)
     pltpu.make_async_copy(weight_in.at[others], weight_in.at[others], weight_recv).wait()
+    weights_in = weight_in[...].reshape(slots, LANES).astype(F32).T.astype(BF16)
     pltpu.make_async_copy(middle.at[others], middle.at[others], one_recv).wait()
 
     held = jnp.concatenate(
         [middle[:, k].astype(F32).reshape(rows * 8, LANES) for k in range(SIDE)], axis=0
     ).astype(BF16)
-    moment = lax.dot_general(
-        weight_in[...].reshape(slots, LANES), held, (((0,), (0,)), ((), ())),
-        preferred_element_type=F32,
-    )
+    moment = dot(weights_in, held)
     part = iota((2 * RANK, LANES), 1) // channels
     moment = sum(
         jnp.where(part == q, moment[q * 2 * RANK : (q + 1) * 2 * RANK], 0.0) for q in range(4)
@@ -297,21 +294,18 @@
     moment_out[...] = packed
     moment_in[rank_in] = packed
 
-    def send_moment(m, carry):
+    for peer in mates:
         pltpu.make_async_remote_copy(
             moment_out, moment_in.at[rank_in], moment_send, moment_recv,
-            device_id=(base + lax.rem(rank_in + m, group), panel), device_id_type=MESH,
+            device_id=(peer, panel), device_id_type=MESH,
         ).start()
-        return carry
-
-    lax.fori_loop(1, group, send_moment, 0, unroll=15)
 
     two = [
         pltpu.make_async_remote_copy(
             middle.at[:, k], recv.at[k], two_send, two_recv,
             device_id=(at(0, k), panel), device_id_type=MESH,
         )
-        for k in range(1, SIDE)
+        for k in far
     ]
     for copy in two:
         copy.start()

time: 34.9 us -> 34.1 us (0.977)
  Pallas kernels: 34.2 us -> 33.4 us
    pallas_call x1, Pallas kernels: 33.5 us -> 32.7 us  [on_device(): pl.pallas_call(functools.partial(body, devices, panels), out_shape=tuple(...]
where the time goes in v4:
time: 34.1 us; the launch traced here: 34 us
  Pallas kernels  33.4 us (98%)
  between operations  0.64 us (2%)
    pallas_call x1, Pallas kernels, on_device(): pl.pallas_call(functools.partial(body, devices, panels), out_shape=tuple(...  32.7 us

profile of v4, /device:TPU:1, one launch (start us, length us, event | category | flops | bytes accessed | tf_op | source)
XLA Modules:
  0.0 34.0 jit_solution(3664235004009383497)
XLA Ops:
  0.6 32.7 %shard_map.120 = (bf16[32,1024]{1,0:T(8,128)(2,1)S(1)}, f32[1,16,32]{2,1,0:T(8,128)S(1)}, f32[1,16,16]{2,1,0:T(8,128)S(1)}, f32[1,16,16]{2,1,0:T(8,128)S(1)}) custom-call(bf16[32,1024]{1,0:T(8,128)(2,1)} %x_hbm.1, s32[8,128]{1,0:T(8,128)} %bitcast.6, s32[64]{0:T(128)} %counts_hbm.1, s32[1,64]{1,0:T(1,128)} %bitcast.7, s32[64]{0:T(128)} %cols_hbm.1, ...), custom_call_target="tpu_custom_call" | custom-call | tf_op jit(solution)/shard_map/pallas_call | solution.py:490
  33.3 0.7 %shard_map.121 = (bf16[32,1024]{1,0:T(8,128)(2,1)}, f32[1,16,32]{2,1,0:T(8,128)}, f32[1,16,16]{2,1,0:T(8,128)}, f32[1,16,16]{2,1,0:T(8,128)}) custom-call(bf16[32,1024]{1,0:T(8,128)(2,1)S(1)} %get-tuple-element.8.refs_0_, f32[1,16,32]{2,1,0:T(8,128)S(1)} %get-tuple-element.9.refs_1_, f32[1,16,16]{2,1,0:T(8,128)S(1)} %get-tuple-element.10.refs_2_, ...), custom_call_target="tpu_custom_call" | custom-call | tf_op jit(solution)/shard_map/pallas_call | solution.py:520

commit v5 on v4

--- a/solution.py
+++ b/solution.py
@@ -300,6 +300,21 @@
             device_id=(peer, panel), device_id_type=MESH,
         ).start()
 
+    peers = pl.ds(0, group - 1)
+    pltpu.make_async_copy(gram_in.at[peers], gram_in.at[peers], gram_recv).wait()
+    sub = iota((RANK, LANES), 0)
+    lane = iota((RANK, LANES), 1)
+    tableau = jnp.where(
+        lane < RANK, unpack2(jnp.sum(gram_in[...], axis=0)), (lane - RANK == sub).astype(F32)
+    )
+    for k in range(RANK - 1):
+        ratio = tableau[:, k : k + 1] / tableau[k : k + 1, k : k + 1]
+        tableau = tableau - jnp.where(sub > k, ratio * tableau[k : k + 1, :], 0.0)
+    pivots = jnp.sum(jnp.where(lane == sub, tableau, 0.0), axis=1, keepdims=True)
+    tableau = tableau * (1.0 / jnp.sqrt(pivots))
+    factor_ref[0] = jnp.where(lane >= sub, tableau, 0.0)[:, :RANK]
+    inverse = tableau[:, RANK : 2 * RANK]
+
     two = [
         pltpu.make_async_remote_copy(
             middle.at[:, k], recv.at[k], two_send, two_recv,
@@ -311,21 +326,6 @@
         copy.start()
     recv[0] = middle[:, 0]
 
-    peers = pl.ds(0, group - 1)
-    pltpu.make_async_copy(gram_in.at[peers], gram_in.at[peers], gram_recv).wait()
-    sub = iota((RANK, LANES), 0)
-    lane = iota((RANK, LANES), 1)
-    tableau = jnp.where(
-        lane < RANK, unpack2(jnp.sum(gram_in[...], axis=0)), (lane - RANK == sub).astype(F32)
-    )
-    for k in range(RANK - 1):
-        ratio = tableau[:, k : k + 1] / tableau[k : k + 1, k : k + 1]
-        tableau = tableau - jnp.where(sub > k, ratio * tableau[k : k + 1, :], 0.0)
-    pivots = jnp.sum(jnp.where(lane == sub, tableau, 0.0), axis=1, keepdims=True)
-    tableau = tableau * (1.0 / jnp.sqrt(pivots))
-    factor_ref[0] = jnp.where(lane >= sub, tableau, 0.0)[:, :RANK]
-    inverse = tableau[:, RANK : 2 * RANK]
-
     pltpu.make_async_copy(moment_in.at[peers], moment_in.at[peers], moment_recv).wait()
     packed = jnp.sum(moment_in[...], axis=0)
     moment = jnp.concatenate(
@@ -333,18 +333,21 @@
     )
     coeffs = dot(inverse, moment, HIGH)
     coeffs_ref[0] = coeffs
-    packed = pack2(dot_t(coeffs, jnp.concatenate([coeffs] * 8, axis=0), HIGH))
+    terms = split3(coeffs)
+    gram = dot_t(
+        jnp.concatenate(terms, axis=0),
+        jnp.concatenate([p for p in terms for _ in range(8)], axis=0),
+    )
+    gram = gram[0:RANK] + gram[RANK : 2 * RANK] + gram[2 * RANK :]
+    packed = pack2(gram[:, 0:LANES] + gram[:, LANES : 2 * LANES] + gram[:, 2 * LANES :])
     top_out[...] = packed
     top_in[panel] = packed
 
-    def send_top(m, carry):
+    for k in sorted(range(1, panels), key=lambda k: -min(k, panels - k)):
         pltpu.make_async_remote_copy(
             top_out, top_in.at[panel], top_send, top_recv,
-            device_id=(me, lax.rem(panel + m, panels)), device_id_type=MESH,
+            device_id=(me, lax.rem(panel + k, panels)), device_id_type=MESH,
         ).start()
-        return carry
-
-    lax.fori_loop(1, panels, send_top, 0, unroll=7)
 
     pltpu.make_async_copy(recv.at[others], recv.at[others], two_recv).wait()
 

time: 34.1 us -> 34 us (level)
  no operation moved by 1% of the time
where the time goes in v5:
time: 34 us; the launch traced here: 33.8 us
  Pallas kernels  33.2 us (98%)
  between operations  0.64 us (2%)
    pallas_call x1, Pallas kernels, on_device(): pl.pallas_call(functools.partial(body, devices, panels), out_shape=tuple(...  32.5 us

profile of v5, /device:TPU:1, one launch (start us, length us, event | category | flops | bytes accessed | tf_op | source)
XLA Modules:
  0.0 33.8 jit_solution(7878350774617234624)
XLA Ops:
  0.6 32.5 %shard_map.120 = (bf16[32,1024]{1,0:T(8,128)(2,1)S(1)}, f32[1,16,32]{2,1,0:T(8,128)S(1)}, f32[1,16,16]{2,1,0:T(8,128)S(1)}, f32[1,16,16]{2,1,0:T(8,128)S(1)}) custom-call(bf16[32,1024]{1,0:T(8,128)(2,1)} %x_hbm.1, s32[8,128]{1,0:T(8,128)} %bitcast.6, s32[64]{0:T(128)} %counts_hbm.1, s32[1,64]{1,0:T(1,128)} %bitcast.7, s32[64]{0:T(128)} %cols_hbm.1, ...), custom_call_target="tpu_custom_call" | custom-call | tf_op jit(solution)/shard_map/pallas_call | solution.py:493
  33.2 0.7 %shard_map.121 = (bf16[32,1024]{1,0:T(8,128)(2,1)}, f32[1,16,32]{2,1,0:T(8,128)}, f32[1,16,16]{2,1,0:T(8,128)}, f32[1,16,16]{2,1,0:T(8,128)}) custom-call(bf16[32,1024]{1,0:T(8,128)(2,1)S(1)} %get-tuple-element.8.refs_0_, f32[1,16,32]{2,1,0:T(8,128)S(1)} %get-tuple-element.9.refs_1_, f32[1,16,16]{2,1,0:T(8,128)S(1)} %get-tuple-element.10.refs_2_, ...), custom_call_target="tpu_custom_call" | custom-call | tf_op jit(solution)/shard_map/pallas_call | solution.py:523

commit v6 on v5

--- a/solution.py
+++ b/solution.py
@@ -313,7 +313,7 @@
     pivots = jnp.sum(jnp.where(lane == sub, tableau, 0.0), axis=1, keepdims=True)
     tableau = tableau * (1.0 / jnp.sqrt(pivots))
     factor_ref[0] = jnp.where(lane >= sub, tableau, 0.0)[:, :RANK]
-    inverse = tableau[:, RANK : 2 * RANK]
+    inverse = jnp.concatenate(split3(tableau[:, RANK : 2 * RANK]), axis=0)
 
     two = [
         pltpu.make_async_remote_copy(
@@ -331,7 +331,8 @@
     moment = jnp.concatenate(
         [packed[:, q * channels : (q + 1) * channels] for q in range(4)], axis=0
     )
-    coeffs = dot(inverse, moment, HIGH)
+    coeffs = sum(dot(inverse, term) for term in split3(moment))
+    coeffs = coeffs[0:RANK] + coeffs[RANK : 2 * RANK] + coeffs[2 * RANK :]
     coeffs_ref[0] = coeffs
     terms = split3(coeffs)
     gram = dot_t(

time: 34 us -> 34 us (level)
  no operation moved by 1% of the time
where the time goes in v6:
time: 34 us; the launch traced here: 33.8 us
  Pallas kernels  33.2 us (98%)
  between operations  0.64 us (2%)
    pallas_call x1, Pallas kernels, on_device(): pl.pallas_call(functools.partial(body, devices, panels), out_shape=tuple(...  32.5 us

profile of v6, /device:TPU:1, one launch (start us, length us, event | category | flops | bytes accessed | tf_op | source)
XLA Modules:
  0.0 33.8 jit_solution(14587421718768579239)
XLA Ops:
  0.6 32.5 %shard_map.120 = (bf16[32,1024]{1,0:T(8,128)(2,1)S(1)}, f32[1,16,32]{2,1,0:T(8,128)S(1)}, f32[1,16,16]{2,1,0:T(8,128)S(1)}, f32[1,16,16]{2,1,0:T(8,128)S(1)}) custom-call(bf16[32,1024]{1,0:T(8,128)(2,1)} %x_hbm.1, s32[8,128]{1,0:T(8,128)} %bitcast.6, s32[64]{0:T(128)} %counts_hbm.1, s32[1,64]{1,0:T(1,128)} %bitcast.7, s32[64]{0:T(128)} %cols_hbm.1, ...), custom_call_target="tpu_custom_call" | custom-call | tf_op jit(solution)/shard_map/pallas_call | solution.py:494
  33.2 0.7 %shard_map.121 = (bf16[32,1024]{1,0:T(8,128)(2,1)}, f32[1,16,32]{2,1,0:T(8,128)}, f32[1,16,16]{2,1,0:T(8,128)}, f32[1,16,16]{2,1,0:T(8,128)}) custom-call(bf16[32,1024]{1,0:T(8,128)(2,1)S(1)} %get-tuple-element.8.refs_0_, f32[1,16,32]{2,1,0:T(8,128)S(1)} %get-tuple-element.9.refs_1_, f32[1,16,16]{2,1,0:T(8,128)S(1)} %get-tuple-element.10.refs_2_, ...), custom_call_target="tpu_custom_call" | custom-call | tf_op jit(solution)/shard_map/pallas_call | solution.py:524
